TPU v7x, 256 devices: a whole 4x4x8 slice. The times are simulated.
256 devices in a mesh: ctx: 16 (over x_lo, y, core), vocab: 16 (over z, x_hi).
Axes of the slice: x: 4 (x_hi: 2, x_lo: 2; x = x_hi * 2 + x_lo), y: 4, z: 8, core: 2. Of those that a mesh axis runs over, the one named last changes fastest.
Arguments:
- query_rows: bfloat16 [8192, 4096], P('ctx', 'vocab'), may hold values from -6 to 6
- key_rows: bfloat16 [8192, 4096], P('ctx', 'vocab'), may hold values from -6 to 6
- value_rows: bfloat16 [8192, 4096], P('ctx', 'vocab'), may hold values from -6 to 6
- log_decay: float32 [32, 8192], P('vocab', 'ctx'), may hold values from -0.75 to 0
- segment_ids: int32 [8192], P('ctx'), may hold values from 0 to 3, as said below
- residual: bfloat16 [8192, 6144], P(('ctx', 'vocab')), may hold values from -20 to 20
- out_weight: bfloat16 [4096, 6144], P('vocab'), may hold values from -0.09375 to 0.09375
- final_gain: float32 [6144], replicated, may hold values from 0.1 to 1.9
- head_weight: bfloat16 [6144, 10240], P(None, 'vocab'), may hold values from -25 to 25
- targets: int32 [8192], P('ctx'), may hold values from 0 to 10239
Outputs:
- log_probs: float32 [8192], P(('ctx', 'vocab'))
Inputs may be any that keep to these rules, and one draw needn't show every extreme that they name: `segment_ids`: never falls; each of the 4 rollouts holds 1 to 4096 tokens, one exactly 4096.
All inputs are finite; a program needn't handle non-finite values.
Results may differ from a plain program's by a relative error of at most 0.02.
Values may be sent and summed in bfloat16 or wider, within the bound.
A program may use at most 128 MiB of HBM per device.

v0:
```python
import jax
import jax.numpy as jnp
from jax import lax
from jax.sharding import PartitionSpec as P

EPSILON = 1e-06


def from_behind(shard, axis, by):
    size = lax.axis_size(axis)
    pairs = [(i, i + by) for i in range(size) if 0 <= i + by < size]
    return lax.ppermute(shard, axis, pairs)


def merged(shard, axis, combine):
    everything = jax.tree.map(lambda part: lax.all_gather(part, axis), shard)
    leading = jax.tree.map(lambda part: part[0], everything)

    def turn(k, so_far):
        return combine(so_far, jax.tree.map(lambda part: part[k], everything))

    return lax.fori_loop(1, lax.axis_size(axis), turn, leading)


def block_terms(query_heads, key_heads, value_heads, log_rates, seg_ids, prior_last):
    row_count = seg_ids.shape[0]
    cumulative = jnp.cumsum(log_rates, axis=1)
    sequence_location = jnp.arange(row_count)
    allowed = (sequence_location[:, None] >= sequence_location[None, :]) & (
        seg_ids[:, None] == seg_ids[None, :]
    )
    spread = cumulative[:, :, None] - cumulative[:, None, :]
    weights = jnp.exp(jnp.where(allowed[None], spread, -jnp.inf))
    scores = jnp.einsum("rhd,shd->hrs", query_heads, key_heads, preferred_element_type=jnp.float32)
    mixing = (scores * weights).astype(jnp.bfloat16)
    within = jnp.einsum("hrs,shd->hrd", mixing, value_heads, preferred_element_type=jnp.float32)
    continues = (seg_ids == prior_last).astype(jnp.float32)
    carry_scale = jnp.exp(cumulative) * continues[None, :]
    tail_weight = (
        jnp.exp(cumulative[:, -1:] - cumulative)
        * (seg_ids == seg_ids[-1]).astype(jnp.float32)[None, :]
    )
    weighted = (key_heads.astype(jnp.float32) * tail_weight.T[:, :, None]).astype(jnp.bfloat16)
    summary = jnp.einsum("rhd,rhe->hde", weighted, value_heads, preferred_element_type=jnp.float32)
    passing = jnp.exp(cumulative[:, -1]) * continues[-1]
    return (within, carry_scale, passing, summary)


def finish_heads(query_heads, within, carry_scale, incoming):
    carried = jnp.einsum(
        "rhd,hde->hre",
        query_heads,
        incoming.astype(jnp.bfloat16),
        preferred_element_type=jnp.float32,
    )
    output = within + carry_scale[:, :, None] * carried
    scaled = output * lax.rsqrt(jnp.mean(output * output, axis=-1, keepdims=True) + EPSILON)
    return jnp.transpose(scaled, (1, 0, 2)).reshape(query_heads.shape[0], -1).astype(jnp.bfloat16)


def final_norm(hidden, final_gain):
    return (
        hidden * lax.rsqrt(jnp.mean(hidden * hidden, axis=1, keepdims=True) + EPSILON) * final_gain
    ).astype(jnp.bfloat16)


def vocab_stats(normed, head_weight, row_targets, offset):
    logits = jnp.dot(normed, head_weight, preferred_element_type=jnp.float32)
    largest = jnp.max(logits, axis=1)
    totals = jnp.sum(jnp.exp(logits - largest[:, None]), axis=1)
    columns = offset + jnp.arange(head_weight.shape[1], dtype=jnp.int32)
    picked = jnp.sum(jnp.where(row_targets[:, None] == columns[None, :], logits, 0.0), axis=1)
    return (largest, totals, picked)


def shards(
    query_rows,
    key_rows,
    value_rows,
    log_decay,
    segment_ids,
    residual,
    out_weight,
    final_gain,
    head_weight,
    targets,
):
    row_count = query_rows.shape[0]
    head_count = log_decay.shape[0]
    head_width = query_rows.shape[1] // head_count
    query_heads = query_rows.reshape(row_count, head_count, head_width)
    key_heads = key_rows.reshape(row_count, head_count, head_width)
    value_heads = value_rows.reshape(row_count, head_count, head_width)
    prior_last = from_behind(segment_ids[-1:], "ctx", 1)[0]
    within, carry_scale, passing, summary = block_terms(
        query_heads, key_heads, value_heads, log_decay, segment_ids, prior_last
    )
    all_passing, all_summary = (
        lax.all_gather(passing[None].astype(jnp.bfloat16), "ctx", axis=0, tiled=True).astype(
            jnp.float32
        ),
        lax.all_gather(summary[None].astype(jnp.bfloat16), "ctx", axis=0, tiled=True).astype(
            jnp.float32
        ),
    )
    ctx_index = lax.axis_index("ctx")

    def absorb(member, running):
        return jnp.where(
            member < ctx_index,
            all_passing[member][:, None, None] * running + all_summary[member],
            running,
        )

    incoming = lax.fori_loop(0, lax.axis_size("ctx"), absorb, jnp.zeros_like(summary))
    attention = finish_heads(query_heads, within, carry_scale, incoming)
    vocab_index = lax.axis_index("vocab")
    offset = vocab_index * head_weight.shape[1]
    row_share = row_count // lax.axis_size("vocab")
    summed = lax.psum_scatter(
        jnp.dot(attention, out_weight, preferred_element_type=jnp.float32).astype(jnp.bfloat16),
        "vocab",
        scatter_dimension=0,
        tiled=True,
    ).astype(jnp.float32)
    normed = final_norm(residual.astype(jnp.float32) + summed, final_gain)
    fresh = vocab_stats(
        lax.all_gather(normed, "vocab", axis=0, tiled=True), head_weight, targets, offset
    )
    largest, totals, picked = tuple((new_stat for new_stat in fresh))
    first_row = vocab_index * row_share

    def combine_stats(left_part, right_part):
        row_top = jnp.maximum(left_part[0], right_part[0])
        merged_total = left_part[1] * jnp.exp(left_part[0] - row_top) + right_part[1] * jnp.exp(
            right_part[0] - row_top
        )
        return (row_top, merged_total, left_part[2] + right_part[2])

    row_top, row_total, target_logit = merged((largest, totals, picked), "vocab", combine_stats)
    result = target_logit - row_top - jnp.log(row_total)
    return lax.dynamic_slice_in_dim(result, first_row, row_share, 0)


def solution(mesh):
    in_specs = (
        P("ctx", "vocab"),
        P("ctx", "vocab"),
        P("ctx", "vocab"),
        P("vocab", "ctx"),
        P("ctx"),
        P(("ctx", "vocab"), None),
        P("vocab", None),
        P(),
        P(None, "vocab"),
        P("ctx"),
    )
    out_specs = P(("ctx", "vocab"))
    return jax.shard_map(shards, mesh=mesh, in_specs=in_specs, out_specs=out_specs, check_vma=False)
```

profile of v0, /device:TPU:24, one launch (start us, length us, event | category | flops | bytes accessed | tf_op | source)
XLA Modules:
  0.0 554.7 jit_solution(16949263543154128033)
XLA Ops:
  6.5 1.4 slice.28
  8.0 1.9 collective-permute-start
  12.4 1.1 copy.36
  13.5 1.9 compare_convert_fusion
  15.5 1.8 convolution_convert_fusion.1
  17.4 1.3 dynamic-slice
  19.3 1.7 fusion.5
  22.5 25.8 %all-reduce = bf16[32]{0:T(256)(128)(2,1)S(1)} all-reduce(bf16[32]{0:T(256)(128)(2,1)S(1)} %dynamic-update-slice), channel_id=2, replica_groups=mesh['ctx'=16,'vocab'=16] {'ctx'}, use_global_device_ids=true, to_apply=%add | all-reduce | flops 32 | bytes 128
  48.4 6.8 %all-gather.13.cloned.1.call-done = bf16[32,128,128]{2,1,0:T(8,128)(2,1)} async-done(((bf16[2,128,128]{2,1,0:T(8,128)(2,1)}), bf16[32,128,128]{2,1,0:T(8,128)(2,1)}) %all-gather.13.cloned.1.call-update) | async-done | bytes 1048592 | tf_op jit(solution)/shard_map/all_gather | solution.py:102
  55.2 2.9 convert
  58.1 16.5 %while.34 = (s32[]{:T(128)}, f32[2,128,128]{2,1,0:T(8,128)S(1)}, s32[]{:T(128)}, f32[16,2]{1,0:T(8,128)S(1)}, f32[16,2,128,128]{3,2,1,0:T(8,128)}, /*index=5*/s32[]{:T(128)}, s32[]{:T(128)}) while((s32[]{:T(128)}, f32[2,128,128]{2,1,0:T(8,128)S(1)}, s32[]{:T(128)}, f32[16,2]{1,0:T(8,128)S(1)}, f32[16,2,128,128]{3,2,1,0:T(8,128)}, ...), condition=%wide.region_3.4_spmd.clone, body=%wide.region_2.3_spmd.clone.sunk | while | flops 131076 | bytes 393345 | solution.py:115
  74.6 1.1 fusion.14
  75.7 3.1 fusion.8
  78.8 1.3 fusion.11
  80.1 4.5 convolution_convert_fusion
  84.7 221.3 %reduce-scatter.2.cloned.1.call-done = bf16[32,6144]{1,0:T(8,128)(2,1)} async-done(((bf16[512,6144]{1,0:T(8,128)(2,1)}), bf16[32,6144]{1,0:T(8,128)(2,1)}) %reduce-scatter.2.cloned.1.call-update) | async-done | bytes 393232 | tf_op jit(solution)/shard_map/reduce_scatter | solution.py:120
  306.0 1.2 multiply_reduce_fusion
  307.3 1.9 multiply_convert_fusion.1
  309.2 114.3 %all-gather.11.cloned.1.call-done = bf16[512,6144]{1,0:T(8,128)(2,1)} async-done(((bf16[32,6144]{1,0:T(8,128)(2,1)}), bf16[512,6144]{1,0:T(8,128)(2,1)}) %all-gather.11.cloned.1.call-update) | async-done | bytes 6291472 | tf_op jit(solution)/shard_map/all_gather | solution.py:128
  423.6 9.6 %fusion.28 = (f32[512]{0:T(512)S(1)}, f32[512,640]{1,0:T(8,128)S(1)}) fusion(bf16[512,6144]{1,0:T(8,128)(2,1)} %all-gather.11.cloned.1.call-done, bf16[6144,640]{1,0:T(8,128)(2,1)} %param.22), kind=kOutput, calls=%fused_computation.57 | convolution fusion | flops 4026859008 | bytes 15468544 | tf_op jit(solution)/shard_map/dot_general | solution.py:68
  433.6 37.6 %all-gather.6 = f32[16,1,512]{2,1,0:T(1,128)S(1)} all-gather(f32[1,1,512]{2,1,0:T(1,128)S(1)} %bitcast.127), channel_id=5, replica_groups=mesh['ctx'=16,'vocab'=16] {'vocab'}, dimensions={0}, use_global_device_ids=true | all-gather | bytes 34816 | tf_op jit(solution)/shard_map/all_gather | solution.py:16
  471.3 37.3 %all-gather.7 = f32[16,1,512]{2,1,0:T(1,128)S(1)} all-gather(f32[1,1,512]{2,1,0:T(1,128)S(1)} %bitcast.126), channel_id=6, replica_groups=mesh['ctx'=16,'vocab'=16] {'vocab'}, dimensions={0}, use_global_device_ids=true | all-gather | bytes 34816 | tf_op jit(solution)/shard_map/all_gather | solution.py:16
  508.5 37.6 %all-gather.5 = f32[16,1,512]{2,1,0:T(1,128)S(1)} all-gather(f32[1,1,512]{2,1,0:T(1,128)S(1)} %bitcast.125), channel_id=4, replica_groups=mesh['ctx'=16,'vocab'=16] {'vocab'}, dimensions={0}, use_global_device_ids=true | all-gather | bytes 34816 | tf_op jit(solution)/shard_map/all_gather | solution.py:16
  546.1 1.4 while.33
  (138 shorter events, 22.2 us)
Async XLA Ops:
  6.5 73.6 %copy-start = (bf16[256,6144]{1,0:T(8,128)(2,1)S(1)}, bf16[256,6144]{1,0:T(8,128)(2,1)}, u32[]{:S(2)}) copy-start(bf16[256,6144]{1,0:T(8,128)(2,1)} %param.20) | copy-start | bytes 9437188
  6.5 48.7 %all-gather.13.cloned.1.call-start = ((), (), s32[]{:S(2)}) async-start(), calls=%async_computation.3 | async-start | bytes 1114112 | tf_op jit(solution)/shard_map/all_gather | solution.py:102
  8.0 5.5 collective-permute-start
  11.6 0.6 copy-start.4
  13.5 3.9 copy-start.3
  17.3 288.7 %reduce-scatter.2.cloned.1.call-start = ((), (), s32[]{:S(2)}) async-start(), calls=%async_computation.1 | async-start | bytes 6684672 | tf_op jit(solution)/shard_map/reduce_scatter | solution.py:120
  55.2 19.4 %copy-start.2 = (bf16[512,256]{1,0:T(8,128)(2,1)S(1)}, bf16[512,256]{1,0:T(8,128)(2,1)}, u32[]{:S(2)}) copy-start(bf16[512,256]{1,0:T(8,128)(2,1)} %param.14) | copy-start | bytes 786436
  84.6 221.4 %copy-start.1 = (bf16[32,6144]{1,0:T(8,128)(2,1)S(1)}, bf16[32,6144]{1,0:T(8,128)(2,1)}, u32[]{:S(2)}) copy-start(bf16[32,6144]{1,0:T(8,128)(2,1)} %param.19) | copy-start | bytes 1179652
  84.6 338.9 %all-gather.11.cloned.1.call-start = ((), (), s32[]{:S(2)}) async-start(), calls=%async_computation.2 | async-start | bytes 6684672 | tf_op jit(solution)/shard_map/all_gather | solution.py:128
  309.2 123.9 %copy-start.5 = (s32[512]{0:T(512)S(1)}, s32[512]{0:T(512)}, u32[]{:S(2)}) copy-start(s32[512]{0:T(512)} %param.23) | copy-start | bytes 6148
Sparse Core Ops, SparseCore 0:
  17.4 37.7 all-gather.12
  84.8 221.2 reduce-scatter.1
  309.3 114.1 all-gather.10
where the time goes:
time: 556 us; the launch traced here: 555 us
  waiting for transfers between devices  343 us (62%)
  blocking collectives  138 us (25%)
  other arithmetic  29.3 us (5%)
  matrix products  20 us (4%)
  between operations  13.9 us (2%)
  local copies, waits for them, and re-layouts  7.48 us (1%)
    reduce_scatter x1, waiting for transfers between devices, shards(): lax.psum_scatter(jnp.dot(attention, out_weight, preferred_element_type=jn...  221 us
    all_gather x1, waiting for transfers between devices, shards(): lax.all_gather(normed, 'vocab', axis=0, tiled=True)  114 us
    all_gather x3, blocking collectives, merged(): everything = jax.tree.map(lambda part: lax.all_gather(part, axis), shard)  112 us
    unnamed x1, blocking collectives  25.8 us
    select_n x16, other arithmetic, absorb(): jnp.where(member < ctx_index, all_passing[member][:, None, None] * runnin...  15.9 us
  transfers between devices with their start and end apart: 4, of which 3 were waited for; matrix products, arithmetic and copies ran while one was open for 1% of the time, Pallas kernels for 0%

commit v1 on v0

v1 whole, which is shorter than its diff:
```python
import jax
import jax.numpy as jnp
from jax import lax
from jax.experimental import pallas as pl
from jax.experimental.pallas import tpu as pltpu
from jax.sharding import PartitionSpec as P

EPSILON = 1e-06
MESH = pl.DeviceIdType.MESH
F32 = jnp.float32
BF16 = jnp.bfloat16

TOK = 512
D = 6144
HD = 128
NV = 640
CH = 32
SUB = 1536
NZ = 8
TILE = 256

SLOT_OFFSET = (0, -1, 1, -2, 2, -3, 3, 4)
GATHER_FROM = ((0, 1, 3, 5), (0, 2, 4, 6))
GATHER_TO = ((1, 3, 5, 7), (2, 4, 6, 7))
SUB_ORDER = ((0, 1, 2, 3), (2, 3, 0, 1))
SUM_SLOTS = ((4, 3, 2, 1), (4, 5, 6, 7))

WO_PIECES = 2
WH_PIECES = 4
WO_PART = 32
WH_PART = 192


def dot(a, b):
    return jnp.dot(a, b, preferred_element_type=F32)


def kernel(
    q_ref, k_ref, v_ref, ld_ref, seg_ref, tgt_ref, res_ref, gain_ref, wo_ref, wh_ref,
    out_ref,
    wo, wh, part, stage, landed, gathered, logits, hidden, within, columns, goals,
    attn, attn_in, lhs, state_out, state_in, stats, stats_in,
    local_sem, piece_send, piece_recv, state_send, state_recv, attn_send, attn_recv,
    sum_send, sum_recv, gather_send, gather_recv, stats_send, stats_recv,
):
    ctx = lax.axis_index("ctx")
    vocab = lax.axis_index("vocab")
    x_lo = ctx // 8
    y = lax.rem(ctx // 2, 4)
    core = lax.rem(ctx, 2)
    z = vocab // 2
    x_hi = lax.rem(vocab, 2)

    def at_y(by):
        return x_lo * 8 + lax.rem(y + by + 4, 4) * 2 + core

    def at_z(by):
        return lax.rem(z + by + NZ, NZ) * 2 + x_hi

    sibling = (ctx + 1 - 2 * core, vocab)
    y_peer = {by: (at_y(by), vocab) for by in (-1, 1, 2)}
    lo_peer = (lax.rem(ctx + 8, 16), vocab)
    cut_peer = (lax.rem(ctx + 8, 16), z * 2 + 1 - x_hi)
    hi_peer = (ctx, z * 2 + 1 - x_hi)
    z_peer = {by: (ctx, at_z(by)) for by in (-3, -2, -1, 1, 2, 3, 4)}

    barrier = pltpu.get_barrier_semaphore()
    peers = [sibling, lo_peer, cut_peer, hi_peer, *y_peer.values(), *z_peer.values()]
    for peer in peers:
        pl.semaphore_signal(barrier, inc=1, device_id=peer, device_id_type=MESH)

    own_wo = pltpu.make_async_copy(wo_ref, wo.at[pl.ds(0, 256)], local_sem.at[0])
    own_wh = pltpu.make_async_copy(wh_ref, wh.at[:, pl.ds(0, NV)], local_sem.at[1])
    own_wo.start()

    waiting = []

    def send(src, dst, send_sem, recv_sem, peer):
        copy = pltpu.make_async_remote_copy(
            src_ref=src, dst_ref=dst, send_sem=send_sem, recv_sem=recv_sem,
            device_id=peer, device_id_type=MESH,
        )
        copy.start()
        waiting.append(copy)
        return copy

    def rows_of(piece, by, of_core, size):
        index = lax.rem(y + by + 4, 4) * 2 + of_core
        if piece < WO_PIECES:
            return pl.multiple_of(index * WO_PART, WO_PART)
        base = (piece - WO_PIECES) * 8 * WH_PART
        return pl.multiple_of(base + index * WH_PART, WH_PART)

    def piece_view(piece, by, low, size):
        start = rows_of(piece, by, core, size) + low
        if piece < WO_PIECES:
            return wo.at[pl.ds(256 + pl.multiple_of(start, 16), size), pl.ds(piece * 3072, 3072)]
        return wh.at[pl.ds(pl.multiple_of(start, 16), size), pl.ds(NV, NV)]

    def piece_source(piece):
        if piece < WO_PIECES:
            rows = pl.ds(rows_of(piece, 0, core, WO_PART), WO_PART)
            return wo_ref.at[rows, pl.ds(piece * 3072, 3072)]
        return wh_ref.at[pl.ds(rows_of(piece, 0, core, WH_PART), WH_PART), :]

    moves = [dict() for _ in range(WO_PIECES + WH_PIECES)]

    def piece_send_to(piece, name, index, src, dst, peer):
        moves[piece][name] = send(
            src, dst, piece_send.at[piece, index], piece_recv.at[piece, index], peer
        )

    def part_size(piece):
        return WO_PART if piece < WO_PIECES else WH_PART

    def fetch_0(piece):
        view = piece_view(piece, 0, 0, part_size(piece))
        piece_send_to(piece, "cut", 0, piece_source(piece), view, cut_peer)

    def fetch_1(piece):
        moves[piece]["cut"].wait_recv()
        view = piece_view(piece, 0, 0, part_size(piece))
        piece_send_to(piece, "up", 1, view, view, y_peer[1])
        piece_send_to(piece, "down", 2, view, view, y_peer[-1])
        piece_send_to(piece, "core0", 5, view, view, sibling)

    def fetch_2(piece):
        size = part_size(piece)
        half = size // 2
        moves[piece]["up"].wait_recv()
        view = piece_view(piece, -1, 0, half)
        piece_send_to(piece, "up2", 3, view, view, y_peer[1])
        view = piece_view(piece, -1, 0, size)
        piece_send_to(piece, "core1", 6, view, view, sibling)
        moves[piece]["down"].wait_recv()
        view = piece_view(piece, 1, half, half)
        piece_send_to(piece, "down2", 4, view, view, y_peer[-1])
        view = piece_view(piece, 1, 0, size)
        piece_send_to(piece, "core2", 7, view, view, sibling)

    def fetch_3(piece):
        moves[piece]["up2"].wait_recv()
        moves[piece]["down2"].wait_recv()
        view = piece_view(piece, 2, 0, part_size(piece))
        piece_send_to(piece, "core3", 8, view, view, sibling)

    def fetch_4(piece):
        for name in ("core0", "core1", "core2", "core3"):
            moves[piece][name].wait_recv()

    lane = lax.broadcasted_iota(jnp.int32, (8, TOK), 1)
    running = jnp.concatenate([ld_ref[...], jnp.zeros((6, TOK), F32)], axis=0)
    shift = 1
    while shift < TOK:
        running = running + jnp.where(lane >= shift, pltpu.roll(running, shift, axis=1), 0.0)
        shift *= 2
    seg_row = seg_ref[...].astype(F32)
    table = jnp.concatenate(
        [running[0:2], seg_row, tgt_ref[...].astype(F32), jnp.zeros((124, TOK), F32)], axis=0
    )
    columns[...] = table.T
    seg_col = columns[:, 2:3]
    seg_last = seg_col[TOK - 1 : TOK, :]

    decay = []
    own_state = []
    for h in range(2):
        head = slice(h * HD, (h + 1) * HD)
        cum_col = columns[:, h : h + 1]
        last = cum_col[TOK - 1 : TOK, :]
        tail = jnp.where(seg_col == seg_last, jnp.exp(last - cum_col), 0.0)
        weighted = (k_ref[:, head].astype(F32) * tail).astype(BF16)
        summary = lax.dot_general(
            weighted, v_ref[:, head], (((0,), (0,)), ((), ())), preferred_element_type=F32
        )
        own_state.append(summary)
        decay.append(jnp.exp(last))

    def pack(slot, states, decays, seg):
        for h in range(2):
            state_out[slot, h * HD : (h + 1) * HD, :] = states[h].astype(BF16)
        row = lax.broadcasted_iota(jnp.int32, (16, HD), 0)
        tops = [d.astype(BF16).astype(F32) for d in decays]
        block = jnp.where(row == 0, tops[0], 0.0)
        block = jnp.where(row == 1, decays[0] - tops[0], block)
        block = jnp.where(row == 2, tops[1], block)
        block = jnp.where(row == 3, decays[1] - tops[1], block)
        block = jnp.where(row == 4, seg, block)
        state_out[slot, 2 * HD : 2 * HD + 16, :] = block.astype(BF16)

    def unpack(buffer, slot):
        states = [buffer[slot, h * HD : (h + 1) * HD, :].astype(F32) for h in range(2)]
        block = buffer[slot, 2 * HD : 2 * HD + 16, :].astype(F32)
        decays = [block[0:1, 0:1] + block[1:2, 0:1], block[2:3, 0:1] + block[3:4, 0:1]]
        return states, decays, block[4:5, 0:1]

    def join(first, second):
        states = [
            jnp.where(first[2] == second[2], second[1][h], 0.0) * first[0][h] + second[0][h]
            for h in range(2)
        ]
        return states, [first[1][h] * second[1][h] for h in range(2)], second[2]

    def choose(flag, a, b):
        return (
            [jnp.where(flag, a[0][h], b[0][h]) for h in range(2)],
            [jnp.where(flag, a[1][h], b[1][h]) for h in range(2)],
            jnp.where(flag, a[2], b[2]),
        )

    pack(0, own_state, decay, seg_last)
    pl.semaphore_wait(barrier, len(peers))
    to_core = send(state_out.at[0], state_in.at[0], state_send.at[0], state_recv.at[0], sibling)
    for piece in range(WO_PIECES):
        fetch_0(piece)

    def inside(h):
        head = slice(h * HD, (h + 1) * HD)
        cum_col = columns[:, h : h + 1]
        cum_row = running[h : h + 1, :]
        for low in (0, 256):
            high = low + 256
            scores = lax.dot_general(
                q_ref[low:high, head], k_ref[0:high, head], (((1,), (1,)), ((), ())),
                preferred_element_type=F32,
            )
            at_row = lax.broadcasted_iota(jnp.int32, (256, high), 0) + low
            at_col = lax.broadcasted_iota(jnp.int32, (256, high), 1)
            allowed = (at_row >= at_col) & (seg_col[low:high] == seg_row[:, 0:high])
            spread = cum_col[low:high] - cum_row[:, 0:high]
            weights = jnp.exp(jnp.where(allowed, spread, -1e30))
            mixing = (scores * weights).astype(BF16)
            within[h, low:high, :] = dot(mixing, v_ref[0:high, head])

    to_core.wait_recv()
    own = unpack(state_out, 0)
    own = (own_state, decay, seg_last)
    other = unpack(state_in, 0)
    first = choose(core == 0, own, other)
    second = choose(core == 0, other, own)
    chip = join(first, second)
    pack(1, *chip)
    to_y = []
    for index, by in enumerate((-1, 1, 2)):
        to_y.append(
            send(
                state_out.at[1], state_in.at[1 + index], state_send.at[1 + index],
                state_recv.at[1 + index], y_peer[by],
            )
        )
    own_wh.start()
    inside(0)
    for copy in to_y:
        copy.wait_recv()
    chips = {0: chip}
    for index, by in enumerate((1, -1, 2)):
        chips[by] = unpack(state_in, 1 + index)

    def chip_at(target):
        picked = chips[0]
        for by in (1, -1, 2):
            picked = choose(lax.rem(y + by + 4, 4) == target, chips[by], picked)
        return picked

    nothing = ([jnp.zeros((HD, HD), F32)] * 2, [jnp.ones((1, 1), F32)] * 2, jnp.zeros((1, 1), F32))
    total = chip_at(0)
    before = choose(y == 0, nothing, total)
    for target in range(1, 4):
        total = join(total, chip_at(target))
        before = choose(y > target, total, before)
    pack(2, *total)
    to_lo = send(state_out.at[2], state_in.at[4], state_send.at[4], state_recv.at[4], lo_peer)
    for piece in range(WO_PIECES):
        fetch_1(piece)
    inside(1)
    to_lo.wait_recv()
    earlier = unpack(state_in, 4)
    joined = choose(y == 0, earlier, join(earlier, before))
    before = choose(x_lo == 0, before, joined)
    fresh = (x_lo == 0) & (y == 0)
    with_first = choose(fresh, first, join(before, first))
    before = choose(core == 0, before, with_first)
    prior = before[2]

    sent_attn = []
    for h in range(2):
        head = slice(h * HD, (h + 1) * HD)
        scale = jnp.where(seg_col == prior, jnp.exp(columns[:, h : h + 1]), 0.0)
        carried = dot(q_ref[:, head], before[0][h].astype(BF16))
        output = within[h] + scale * carried
        mean = jnp.mean(output * output, axis=-1, keepdims=True)
        scaled = (output * lax.rsqrt(mean + EPSILON)).astype(BF16)
        for j in range(NZ):
            for half in range(2):
                low = (2 * j + half) * CH
                attn[h, half, j] = scaled[low : low + CH]
        sent_attn.append(
            send(attn.at[h, 1 - x_hi], attn_in.at[h], attn_send.at[h], attn_recv.at[h], hi_peer)
        )
    for piece in range(WO_PIECES):
        fetch_2(piece)
    for piece in range(WO_PIECES, WO_PIECES + WH_PIECES):
        fetch_0(piece)
    for d in range(NZ):
        chunk = lax.rem(z + d, NZ)
        rows = slice(d * CH, (d + 1) * CH)
        for h in range(2):
            lhs[rows, h * HD : (h + 1) * HD] = attn[h, x_hi, chunk]
    for slot, offset in enumerate(SLOT_OFFSET):
        chunk = lax.rem(z + offset + NZ, NZ)
        rows = pl.ds(pl.multiple_of((2 * chunk + x_hi) * CH, CH), CH)
        goals[slot * CH : (slot + 1) * CH, :] = columns[rows, :]
    for copy in sent_attn:
        copy.wait_recv()
    for d in range(NZ):
        chunk = lax.rem(z + d, NZ)
        rows = slice(d * CH, (d + 1) * CH)
        for h in range(2):
            lhs[rows, 256 + h * HD : 256 + (h + 1) * HD] = attn_in[h, chunk]
    for piece in range(WO_PIECES):
        fetch_3(piece)
    own_wo.wait()
    for piece in range(WO_PIECES):
        fetch_4(piece)

    def project(sub):
        def tile(t, carry):
            cols = pl.ds(pl.multiple_of(sub * SUB + t * 512, 512), 512)
            part[:, :, cols] = dot(lhs[...], wo[:, cols]).reshape(NZ, CH, 512)
            return carry

        lax.fori_loop(0, SUB // 512, tile, 0)

    sums = {}

    def sum_send_to(way, step, sub):
        cols = slice(sub * SUB, (sub + 1) * SUB)
        value = part[SUM_SLOTS[way][step], :, cols]
        if (way, step - 1, sub) in sums:
            sums[way, step - 1, sub].wait_recv()
            value = value + landed[way, step - 1, :, cols].astype(F32)
        stage[way, step, :, cols] = value.astype(BF16)
        index = (way * 4 + step) * 4 + sub
        sums[way, step, sub] = send(
            stage.at[way, step, :, pl.ds(sub * SUB, SUB)],
            landed.at[way, step, :, pl.ds(sub * SUB, SUB)],
            sum_send.at[index], sum_recv.at[index], z_peer[1 if way == 0 else -1],
        )

    for i in range(2):
        for way in range(2):
            project(SUB_ORDER[way][i])
            sum_send_to(way, 0, SUB_ORDER[way][i])
    service = [
        lambda: fetch_1(2),
        lambda: fetch_1(3),
        lambda: fetch_2(2),
        lambda: (fetch_1(4), fetch_2(3)),
        lambda: (fetch_1(5), fetch_3(2)),
        lambda: (fetch_2(4), fetch_3(3)),
        lambda: fetch_2(5),
    ]
    count = 0
    for step in range(1, 4):
        for i in (2, 3, 0, 1):
            for way in range(2):
                sum_send_to(way, step, SUB_ORDER[way][i])
            count += 1
            if count >= 5 and service:
                service.pop(0)()
    while service:
        service.pop(0)()

    square = jnp.zeros((CH, 1), F32)
    for i in (2, 0, 3, 1):
        sub = i
        cols = slice(sub * SUB, (sub + 1) * SUB)
        for way in range(2):
            sums[way, 3, sub].wait_recv()
        value = part[0, :, cols] + landed[0, 3, :, cols].astype(F32)
        value = value + landed[1, 3, :, cols].astype(F32) + res_ref[:, cols].astype(F32)
        hidden[:, cols] = value
        square = square + jnp.sum(value * value, axis=1, keepdims=True)
    scale = lax.rsqrt(square / D + EPSILON)

    gathers = {}

    def gather_to(way, step, sub):
        if step > 0:
            gathers[way, step - 1, sub].wait_recv()
        src = GATHER_FROM[way][step] * CH
        dst = GATHER_TO[way][step] * CH
        cols = pl.ds(sub * SUB, SUB)
        index = (way * 4 + step) * 4 + sub
        gathers[way, step, sub] = send(
            gathered.at[pl.ds(src, CH), cols], gathered.at[pl.ds(dst, CH), cols],
            gather_send.at[index], gather_recv.at[index], z_peer[1 if way == 0 else -1],
        )

    for sub in (0, 2, 1, 3):
        cols = slice(sub * SUB, (sub + 1) * SUB)
        gathered[0:CH, cols] = (hidden[:, cols] * scale * gain_ref[:, cols]).astype(BF16)
        for way in range(2):
            gather_to(way, 0, sub)

    own_wh.wait()
    own_offset = vocab * NV
    other_offset = (z * 2 + 1 - x_hi) * NV

    def multiply(first, count, tile):
        rows = slice(first * CH, (first + count) * CH)
        cols = slice(tile * TILE, (tile + 1) * TILE)
        logits[rows, cols] = dot(gathered[rows, :], wh[:, cols])

    def summarize(first, count):
        size = count * CH
        rows = slice(first * CH, (first + count) * CH)
        values = logits[rows, :]
        top = jnp.max(values, axis=1, keepdims=True)
        mass = jnp.sum(jnp.exp(values - top), axis=1, keepdims=True)
        column = lax.broadcasted_iota(jnp.int32, (size, 2 * NV), 1)
        column = jnp.where(column < NV, column + own_offset, column - NV + other_offset)
        goal = goals[rows, 3:4].astype(jnp.int32)
        hit = jnp.sum(jnp.where(column == goal, values, 0.0), axis=1, keepdims=True)
        place = lax.broadcasted_iota(jnp.int32, (size, HD), 1)
        block = jnp.where(place == 0, top, jnp.where(place == 1, mass, hit))
        stats[rows, :] = block
        for slot in range(first, first + count):
            if slot > 0:
                stats_moves[slot] = send(
                    stats.at[pl.ds(slot * CH, CH)], stats_in.at[slot],
                    stats_send.at[slot], stats_recv.at[slot], z_peer[SLOT_OFFSET[slot]],
                )

    stats_moves = {}
    fetch_3(4)
    fetch_3(5)
    for i in range(4):
        for way in range(2):
            gather_to(way, 1, SUB_ORDER[way][i])
    for piece in range(WO_PIECES, WO_PIECES + WH_PIECES):
        fetch_4(piece)
    for i in range(4):
        multiply(0, 3, i)
        for way in range(2):
            gather_to(way, 2, SUB_ORDER[way][i])
    multiply(0, 3, 4)
    summarize(0, 3)
    for i in range(2):
        multiply(3, 2, i)
        for way in range(2):
            gather_to(way, 3, SUB_ORDER[way][i])
    for i in range(2, 5):
        multiply(3, 2, i)
    summarize(3, 2)
    for way in range(2):
        for i in range(2, 4):
            gathers[way, 2, SUB_ORDER[way][i]].wait_recv()
        for i in range(2):
            gathers[way, 3, SUB_ORDER[way][i]].wait_recv()
    for i in range(5):
        multiply(5, 3, i)
    summarize(5, 3)

    blocks = [stats[0:CH, :]]
    for slot in range(1, NZ):
        stats_moves[slot].wait_recv()
        blocks.append(stats_in[slot])
    top = blocks[0][:, 0:1]
    for block in blocks[1:]:
        top = jnp.maximum(top, block[:, 0:1])
    mass = jnp.zeros((CH, 1), F32)
    hit = jnp.zeros((CH, 1), F32)
    for block in blocks:
        mass = mass + block[:, 1:2] * jnp.exp(block[:, 0:1] - top)
        hit = hit + block[:, 2:3]
    result = jnp.broadcast_to(hit - top - jnp.log(mass), (CH, HD))
    padded = jnp.concatenate([result, jnp.zeros((HD - CH, HD), F32)], axis=0)
    out_ref[...] = padded.T[0:1, 0:CH]
    for copy in waiting:
        copy.wait_send()


def shards(
    query_rows, key_rows, value_rows, log_decay, segment_ids, residual, out_weight, final_gain,
    head_weight, targets,
):
    vmem = pl.BlockSpec(memory_space=pltpu.VMEM)
    hbm = pl.BlockSpec(memory_space=pl.ANY)
    dma = pltpu.SemaphoreType.DMA
    pieces = WO_PIECES + WH_PIECES
    result = pl.pallas_call(
        kernel,
        out_shape=jax.ShapeDtypeStruct((1, CH), F32),
        in_specs=[vmem] * 8 + [hbm] * 2,
        out_specs=vmem,
        scratch_shapes=[
            pltpu.VMEM((512, D), BF16),
            pltpu.VMEM((D, 2 * NV), BF16),
            pltpu.VMEM((NZ, CH, D), F32),
            pltpu.VMEM((2, 4, CH, D), BF16),
            pltpu.VMEM((2, 4, CH, D), BF16),
            pltpu.VMEM((NZ * CH, D), BF16),
            pltpu.VMEM((NZ * CH, 2 * NV), F32),
            pltpu.VMEM((CH, D), F32),
            pltpu.VMEM((2, TOK, HD), F32),
            pltpu.VMEM((TOK, HD), F32),
            pltpu.VMEM((NZ * CH, HD), F32),
            pltpu.VMEM((2, 2, NZ, CH, HD), BF16),
            pltpu.VMEM((2, NZ, CH, HD), BF16),
            pltpu.VMEM((NZ * CH, 512), BF16),
            pltpu.VMEM((3, 2 * HD + 16, HD), BF16),
            pltpu.VMEM((5, 2 * HD + 16, HD), BF16),
            pltpu.VMEM((NZ * CH, HD), F32),
            pltpu.VMEM((NZ, CH, HD), F32),
            dma((2,)),
            dma((pieces, 9)),
            dma((pieces, 9)),
            dma((5,)),
            dma((5,)),
            dma((2,)),
            dma((2,)),
            dma((32,)),
            dma((32,)),
            dma((32,)),
            dma((32,)),
            dma((NZ,)),
            dma((NZ,)),
        ],
        compiler_params=pltpu.CompilerParams(
            collective_id=0, has_side_effects=True, vmem_limit_bytes=56 * 1024 * 1024
        ),
        name="layer",
    )(
        query_rows, key_rows, value_rows, log_decay, segment_ids.reshape(1, -1),
        targets.reshape(1, -1), residual, final_gain.reshape(1, -1), out_weight, head_weight,
    )
    return result.reshape(CH)


def solution(mesh):
    in_specs = (
        P("ctx", "vocab"),
        P("ctx", "vocab"),
        P("ctx", "vocab"),
        P("vocab", "ctx"),
        P("ctx"),
        P(("ctx", "vocab"), None),
        P("vocab", None),
        P(),
        P(None, "vocab"),
        P("ctx"),
    )
    out_specs = P(("ctx", "vocab"))
    return jax.shard_map(shards, mesh=mesh, in_specs=in_specs, out_specs=out_specs, check_vma=False)
```

time: 556 us -> 123 us (0.22)
  waiting for transfers between devices: 343 us -> 0 us
  blocking collectives: 138 us -> 0 us
  Pallas kernels: 0 us -> 120 us
  other arithmetic: 29.3 us -> 0 us
  matrix products: 20 us -> 0 us
  between operations: 13.9 us -> 0.01 us
  local copies, waits for them, and re-layouts: 7.48 us -> 1.19 us
    reduce_scatter x1 -> x0, waiting for transfers between devices: 221 us -> none  [shards(): lax.psum_scatter(jnp.dot(attention, out_weight, preferred_element_type=jn...]
    all_gather x2 -> x0, waiting for transfers between devices: 121 us -> none  [the longest x1 114 us: shards(): lax.all_gather(normed, 'vocab', axis=0, tiled=True)]
    pallas_call x0 -> x1, Pallas kernels: none -> 120 us  [shards(): pl.pallas_call(kernel, out_shape=jax.ShapeDtypeStruct((1, CH), F32), in_s...]
    all_gather x3 -> x0, blocking collectives: 112 us -> none  [merged(): everything = jax.tree.map(lambda part: lax.all_gather(part, axis), shard)]
    unnamed x1 -> x0, blocking collectives: 25.8 us -> none
    dot_general x5 -> x0, matrix products: 20 us -> none  [the longest x1 9.58 us: vocab_stats(): logits = jnp.dot(normed, head_weight, preferred_element_type=jnp.float32)]
    select_n x16 -> x0, other arithmetic: 15.9 us -> none  [absorb(): jnp.where(member < ctx_index, all_passing[member][:, None, None] * runnin...]
    convert_element_type x4 -> x0, other arithmetic: 8.03 us -> none  [the longest x1 2.86 us: shards(): lax.all_gather(summary[None].astype(jnp.bfloat16), 'ctx', axis=0, tiled=T...]
  transfers between devices with their start and end apart: 4 -> 0, of which waited for: 3 -> 0; matrix products, arithmetic and copies ran while one was open for 1% -> 0% of each run, Pallas kernels for 0% -> 0%
where the time goes in v1:
time: 123 us; the launch traced here: 121 us
  Pallas kernels  120 us (98%)
    pallas_call x1, Pallas kernels, shards(): pl.pallas_call(kernel, out_shape=jax.ShapeDtypeStruct((1, CH), F32), in_s...  120 us

profile of v1, /device:TPU:24, one launch (start us, length us, event | category | flops | bytes accessed | tf_op | source)
XLA Modules:
  0.0 121.0 jit_solution(18110440670606473925)
XLA Ops:
  0.0 119.8 %layer.1 = f32[1,32]{1,0:T(1,128)} custom-call(bf16[512,256]{1,0:T(8,128)(2,1)} %q_ref.1, bf16[512,256]{1,0:T(8,128)(2,1)} %k_ref.1, bf16[512,256]{1,0:T(8,128)(2,1)} %v_ref.1, f32[2,512]{1,0:T(2,128)} %ld_ref.1, s32[1,512]{1,0:T(1,128)} %bitcast.5, s32[1,512]{1,0:T(1,128)} %bitcast.6, bf16[32,6144]{1,0:T(8,128)(2,1)} %res_ref.1, f32[1,6144]{1,0:T(1,128)} %bitcast.4, ...), custom_call_target="tpu_custom_call" | custom-call | tf_op jit(solution)/shard_map/layer/pallas_call | solution.py:492
  119.8 1.2 copy.12

commit v2 on v1

--- a/solution.py
+++ b/solution.py
@@ -25,10 +25,12 @@
 SUB_ORDER = ((0, 1, 2, 3), (2, 3, 0, 1))
 SUM_SLOTS = ((4, 3, 2, 1), (4, 5, 6, 7))
 
-WO_PIECES = 2
-WH_PIECES = 4
-WO_PART = 32
-WH_PART = 192
+WO_ORDER = (0, 2, 1, 3)
+KINDS = "YYXY" "YYYYYX"
+WO_PIECES = 4
+WH_PIECES = 6
+WO_ROWS = 256
+WH_ROWS = 1024
 
 
 def dot(a, b):
@@ -36,12 +38,13 @@
 
 
 def kernel(
-    q_ref, k_ref, v_ref, ld_ref, seg_ref, tgt_ref, res_ref, gain_ref, wo_ref, wh_ref,
+    q_hbm, k_hbm, v_hbm, ld_hbm, seg_hbm, tgt_hbm, res_hbm, gain_hbm, wo_ref, wh_ref,
     out_ref,
-    wo, wh, part, stage, landed, gathered, logits, hidden, within, columns, goals,
+    q_ref, k_ref, v_ref, ld_ref, seg_ref, tgt_ref, res_ref, gain_ref,
+    wo, wh, part, stage, landed, gathered, logits, scales, within, columns, goals,
     attn, attn_in, lhs, state_out, state_in, stats, stats_in,
     local_sem, piece_send, piece_recv, state_send, state_recv, attn_send, attn_recv,
-    sum_send, sum_recv, gather_send, gather_recv, stats_send, stats_recv,
+    sum_send, sum_recv, gather_send, gather_recv, scale_send, scale_recv, stats_send, stats_recv,
 ):
     ctx = lax.axis_index("ctx")
     vocab = lax.axis_index("vocab")
@@ -69,9 +72,17 @@
     for peer in peers:
         pl.semaphore_signal(barrier, inc=1, device_id=peer, device_id_type=MESH)
 
-    own_wo = pltpu.make_async_copy(wo_ref, wo.at[pl.ds(0, 256)], local_sem.at[0])
-    own_wh = pltpu.make_async_copy(wh_ref, wh.at[:, pl.ds(0, NV)], local_sem.at[1])
-    own_wo.start()
+    def load(index, src, dst):
+        copy = pltpu.make_async_copy(src, dst, local_sem.at[index])
+        copy.start()
+        return copy
+
+    small = [
+        load(0, ld_hbm, ld_ref), load(1, seg_hbm, seg_ref), load(2, tgt_hbm, tgt_ref),
+        load(3, k_hbm, k_ref), load(4, v_hbm, v_ref),
+    ]
+    load_q = load(5, q_hbm, q_ref)
+    own_wo = load(6, wo_ref, wo.at[pl.ds(0, 256)])
 
     waiting = []
 
@@ -84,70 +95,89 @@
         waiting.append(copy)
         return copy
 
-    def rows_of(piece, by, of_core, size):
-        index = lax.rem(y + by + 4, 4) * 2 + of_core
+    def part_rows(piece):
+        rows = WO_ROWS if piece < WO_PIECES else WH_ROWS
+        return rows // (8 if KINDS[piece] == "Y" else 4)
+
+    def part_start(piece, by):
+        size = part_rows(piece)
+        if KINDS[piece] == "Y":
+            start = (lax.rem(y + by + 4, 4) * 2 + core) * size
+        else:
+            start = (lax.rem(x_lo + by, 2) * 2 + core) * size
+        if piece >= WO_PIECES:
+            start = start + (piece - WO_PIECES) * WH_ROWS
+        return start
+
+    def piece_view(piece, by, low=0, size=None):
+        start = part_start(piece, by) + low
+        size = part_rows(piece) if size is None else size
         if piece < WO_PIECES:
-            return pl.multiple_of(index * WO_PART, WO_PART)
-        base = (piece - WO_PIECES) * 8 * WH_PART
-        return pl.multiple_of(base + index * WH_PART, WH_PART)
-
-    def piece_view(piece, by, low, size):
-        start = rows_of(piece, by, core, size) + low
+            cols = pl.ds(WO_ORDER[piece] * SUB, SUB)
+            return wo.at[pl.ds(WO_ROWS + pl.multiple_of(start, 16), size), cols]
+        return wh.at[pl.ds(pl.multiple_of(start, 16), size), pl.ds(NV, NV)]
+
+    def piece_source(piece):
+        rows = pl.ds(pl.multiple_of(part_start_other(piece), 16), part_rows(piece))
         if piece < WO_PIECES:
-            return wo.at[pl.ds(256 + pl.multiple_of(start, 16), size), pl.ds(piece * 3072, 3072)]
-        return wh.at[pl.ds(pl.multiple_of(start, 16), size), pl.ds(NV, NV)]
-
-    def piece_source(piece):
-        if piece < WO_PIECES:
-            rows = pl.ds(rows_of(piece, 0, core, WO_PART), WO_PART)
-            return wo_ref.at[rows, pl.ds(piece * 3072, 3072)]
-        return wh_ref.at[pl.ds(rows_of(piece, 0, core, WH_PART), WH_PART), :]
+            return wo_ref.at[rows, pl.ds(WO_ORDER[piece] * SUB, SUB)]
+        return wh_ref.at[rows, :]
+
+    def part_start_other(piece):
+        return part_start(piece, 0 if KINDS[piece] == "Y" else 1)
 
     moves = [dict() for _ in range(WO_PIECES + WH_PIECES)]
 
-    def piece_send_to(piece, name, index, src, dst, peer):
+    def piece_move(piece, name, index, src, dst, peer):
         moves[piece][name] = send(
             src, dst, piece_send.at[piece, index], piece_recv.at[piece, index], peer
         )
 
-    def part_size(piece):
-        return WO_PART if piece < WO_PIECES else WH_PART
-
     def fetch_0(piece):
-        view = piece_view(piece, 0, 0, part_size(piece))
-        piece_send_to(piece, "cut", 0, piece_source(piece), view, cut_peer)
+        there = piece_view(piece, 0 if KINDS[piece] == "Y" else 1)
+        piece_move(piece, "cut", 0, piece_source(piece), there, cut_peer)
 
     def fetch_1(piece):
         moves[piece]["cut"].wait_recv()
-        view = piece_view(piece, 0, 0, part_size(piece))
-        piece_send_to(piece, "up", 1, view, view, y_peer[1])
-        piece_send_to(piece, "down", 2, view, view, y_peer[-1])
-        piece_send_to(piece, "core0", 5, view, view, sibling)
+        view = piece_view(piece, 0)
+        if KINDS[piece] == "Y":
+            piece_move(piece, "up", 1, view, view, y_peer[1])
+            piece_move(piece, "down", 2, view, view, y_peer[-1])
+        else:
+            piece_move(piece, "lo", 1, view, view, lo_peer)
+        piece_move(piece, "core0", 5, view, view, sibling)
 
     def fetch_2(piece):
-        size = part_size(piece)
-        half = size // 2
+        if KINDS[piece] == "X":
+            moves[piece]["lo"].wait_recv()
+            view = piece_view(piece, 1)
+            piece_move(piece, "core1", 6, view, view, sibling)
+            return
+        half = part_rows(piece) // 2
         moves[piece]["up"].wait_recv()
         view = piece_view(piece, -1, 0, half)
-        piece_send_to(piece, "up2", 3, view, view, y_peer[1])
-        view = piece_view(piece, -1, 0, size)
-        piece_send_to(piece, "core1", 6, view, view, sibling)
+        piece_move(piece, "up2", 3, view, view, y_peer[1])
+        view = piece_view(piece, -1)
+        piece_move(piece, "core1", 6, view, view, sibling)
         moves[piece]["down"].wait_recv()
         view = piece_view(piece, 1, half, half)
-        piece_send_to(piece, "down2", 4, view, view, y_peer[-1])
-        view = piece_view(piece, 1, 0, size)
-        piece_send_to(piece, "core2", 7, view, view, sibling)
+        piece_move(piece, "down2", 4, view, view, y_peer[-1])
+        view = piece_view(piece, 1)
+        piece_move(piece, "core2", 7, view, view, sibling)
 
     def fetch_3(piece):
         moves[piece]["up2"].wait_recv()
         moves[piece]["down2"].wait_recv()
-        view = piece_view(piece, 2, 0, part_size(piece))
-        piece_send_to(piece, "core3", 8, view, view, sibling)
+        view = piece_view(piece, 2)
+        piece_move(piece, "core3", 8, view, view, sibling)
 
     def fetch_4(piece):
         for name in ("core0", "core1", "core2", "core3"):
-            moves[piece][name].wait_recv()
-
+            if name in moves[piece]:
+                moves[piece][name].wait_recv()
+
+    for copy in small:
+        copy.wait()
     lane = lax.broadcasted_iota(jnp.int32, (8, TOK), 1)
     running = jnp.concatenate([ld_ref[...], jnp.zeros((6, TOK), F32)], axis=0)
     shift = 1
@@ -248,8 +278,14 @@
                 state_recv.at[1 + index], y_peer[by],
             )
         )
-    own_wh.start()
+    load_res = load(7, res_hbm, res_ref)
+    load_gain = load(8, gain_hbm, gain_ref)
+    own_wh = load(9, wh_ref, wh.at[:, pl.ds(0, NV)])
+    load_q.wait()
     inside(0)
+    inside(1)
+    fetch_1(0)
+    fetch_1(1)
     for copy in to_y:
         copy.wait_recv()
     chips = {0: chip}
@@ -270,9 +306,7 @@
         before = choose(y > target, total, before)
     pack(2, *total)
     to_lo = send(state_out.at[2], state_in.at[4], state_send.at[4], state_recv.at[4], lo_peer)
-    for piece in range(WO_PIECES):
-        fetch_1(piece)
-    inside(1)
+    fetch_2(0)
     to_lo.wait_recv()
     earlier = unpack(state_in, 4)
     joined = choose(y == 0, earlier, join(earlier, before))
@@ -297,10 +331,10 @@
         sent_attn.append(
             send(attn.at[h, 1 - x_hi], attn_in.at[h], attn_send.at[h], attn_recv.at[h], hi_peer)
         )
-    for piece in range(WO_PIECES):
-        fetch_2(piece)
-    for piece in range(WO_PIECES, WO_PIECES + WH_PIECES):
-        fetch_0(piece)
+    fetch_2(1)
+    fetch_1(2)
+    fetch_3(0)
+    fetch_1(3)
     for d in range(NZ):
         chunk = lax.rem(z + d, NZ)
         rows = slice(d * CH, (d + 1) * CH)
@@ -312,16 +346,16 @@
         goals[slot * CH : (slot + 1) * CH, :] = columns[rows, :]
     for copy in sent_attn:
         copy.wait_recv()
+    for piece in range(WO_PIECES, WO_PIECES + WH_PIECES):
+        fetch_0(piece)
     for d in range(NZ):
         chunk = lax.rem(z + d, NZ)
         rows = slice(d * CH, (d + 1) * CH)
         for h in range(2):
             lhs[rows, 256 + h * HD : 256 + (h + 1) * HD] = attn_in[h, chunk]
-    for piece in range(WO_PIECES):
-        fetch_3(piece)
     own_wo.wait()
-    for piece in range(WO_PIECES):
-        fetch_4(piece)
+    fetch_3(1)
+    fetch_4(0)
 
     def project(sub):
         def tile(t, carry):
@@ -330,6 +364,10 @@
             return carry
 
         lax.fori_loop(0, SUB // 512, tile, 0)
+
+    def as_row(column):
+        wide = jnp.broadcast_to(column, (CH, HD))
+        return jnp.concatenate([wide, jnp.zeros((HD - CH, HD), F32)], axis=0).T
 
     sums = {}
 
@@ -347,41 +385,40 @@
             sum_send.at[index], sum_recv.at[index], z_peer[1 if way == 0 else -1],
         )
 
-    for i in range(2):
-        for way in range(2):
-            project(SUB_ORDER[way][i])
-            sum_send_to(way, 0, SUB_ORDER[way][i])
-    service = [
-        lambda: fetch_1(2),
-        lambda: fetch_1(3),
-        lambda: fetch_2(2),
-        lambda: (fetch_1(4), fetch_2(3)),
-        lambda: (fetch_1(5), fetch_3(2)),
-        lambda: (fetch_2(4), fetch_3(3)),
-        lambda: fetch_2(5),
-    ]
-    count = 0
+    project(0)
+    sum_send_to(0, 0, 0)
+    sum_send_to(1, 1, 0)
+    fetch_2(2)
+    fetch_4(1)
+    project(2)
+    sum_send_to(1, 0, 2)
+    sum_send_to(0, 1, 2)
+    fetch_2(3)
+    fetch_4(2)
+    project(1)
+    sum_send_to(0, 0, 1)
+    sum_send_to(1, 1, 1)
+    fetch_3(3)
+    fetch_4(3)
+    project(3)
+    sum_send_to(1, 0, 3)
+    sum_send_to(0, 1, 3)
+    fetch_1(4)
+    service = {
+        3: [(fetch_1, 5)],
+        6: [(fetch_2, 4), (fetch_1, 6)],
+        8: [(fetch_2, 5), (fetch_1, 7)],
+        9: [(fetch_1, 8)],
+        10: [(fetch_3, 4), (fetch_2, 6)],
+    }
+    count = 2
     for step in range(1, 4):
-        for i in (2, 3, 0, 1):
+        for i in (2, 3, 0, 1) if step > 1 else (0, 1):
             for way in range(2):
                 sum_send_to(way, step, SUB_ORDER[way][i])
+            for fetch, piece in service.get(count, ()):
+                fetch(piece)
             count += 1
-            if count >= 5 and service:
-                service.pop(0)()
-    while service:
-        service.pop(0)()
-
-    square = jnp.zeros((CH, 1), F32)
-    for i in (2, 0, 3, 1):
-        sub = i
-        cols = slice(sub * SUB, (sub + 1) * SUB)
-        for way in range(2):
-            sums[way, 3, sub].wait_recv()
-        value = part[0, :, cols] + landed[0, 3, :, cols].astype(F32)
-        value = value + landed[1, 3, :, cols].astype(F32) + res_ref[:, cols].astype(F32)
-        hidden[:, cols] = value
-        square = square + jnp.sum(value * value, axis=1, keepdims=True)
-    scale = lax.rsqrt(square / D + EPSILON)
 
     gathers = {}
 
@@ -397,25 +434,55 @@
             gather_send.at[index], gather_recv.at[index], z_peer[1 if way == 0 else -1],
         )
 
-    for sub in (0, 2, 1, 3):
+    square = jnp.zeros((CH, 1), F32)
+    load_res.wait()
+    load_gain.wait()
+    for sub in (2, 0, 3, 1):
         cols = slice(sub * SUB, (sub + 1) * SUB)
-        gathered[0:CH, cols] = (hidden[:, cols] * scale * gain_ref[:, cols]).astype(BF16)
+        for way in range(2):
+            sums[way, 3, sub].wait_recv()
+        value = part[0, :, cols] + landed[0, 3, :, cols].astype(F32)
+        value = value + landed[1, 3, :, cols].astype(F32) + res_ref[:, cols].astype(F32)
+        gathered[0:CH, cols] = (value * gain_ref[:, cols]).astype(BF16)
         for way in range(2):
             gather_to(way, 0, sub)
+        square = square + jnp.sum(value * value, axis=1, keepdims=True)
+    scale = lax.rsqrt(square / D + EPSILON)
+    scales[0] = as_row(scale)[0:8, :]
+    scale_moves = {}
+    for slot in range(1, NZ):
+        scale_moves[slot] = send(
+            scales.at[0], scales.at[slot], scale_send.at[slot], scale_recv.at[slot],
+            z_peer[SLOT_OFFSET[slot] if slot == NZ - 1 else -SLOT_OFFSET[slot]],
+        )
 
     own_wh.wait()
     own_offset = vocab * NV
     other_offset = (z * 2 + 1 - x_hi) * NV
 
-    def multiply(first, count, tile):
+    def multiply(first, count, tile, subs=None, more=False):
         rows = slice(first * CH, (first + count) * CH)
         cols = slice(tile * TILE, (tile + 1) * TILE)
-        logits[rows, cols] = dot(gathered[rows, :], wh[:, cols])
+        if subs is None:
+            logits[rows, cols] = dot(gathered[rows, :], wh[:, cols])
+            return
+        value = logits[rows, cols] if more else 0.0
+        for sub in subs:
+            deep = slice(sub * SUB, (sub + 1) * SUB)
+            value = value + dot(gathered[rows, deep], wh[deep, cols])
+        logits[rows, cols] = value
 
     def summarize(first, count):
         size = count * CH
         rows = slice(first * CH, (first + count) * CH)
-        values = logits[rows, :]
+        lines = []
+        for slot in range(first, first + count):
+            if slot > 0:
+                scale_moves[slot].wait_recv()
+            lines.append(scales[slot, 0:1, :])
+        table = jnp.concatenate(lines + [jnp.zeros((HD - count, HD), F32)], axis=0).T
+        factor = jnp.concatenate([table[0:CH, i : i + 1] for i in range(count)], axis=0)
+        values = logits[rows, :] * factor
         top = jnp.max(values, axis=1, keepdims=True)
         mass = jnp.sum(jnp.exp(values - top), axis=1, keepdims=True)
         column = lax.broadcasted_iota(jnp.int32, (size, 2 * NV), 1)
@@ -433,11 +500,20 @@
                 )
 
     stats_moves = {}
-    fetch_3(4)
+    fetch_2(7)
+    fetch_1(9)
     fetch_3(5)
+    fetch_3(6)
+    fetch_2(8)
     for i in range(4):
         for way in range(2):
             gather_to(way, 1, SUB_ORDER[way][i])
+        if i == 0:
+            fetch_3(7)
+        if i == 1:
+            fetch_3(8)
+        if i == 2:
+            fetch_2(9)
     for piece in range(WO_PIECES, WO_PIECES + WH_PIECES):
         fetch_4(piece)
     for i in range(4):
@@ -456,10 +532,11 @@
     for way in range(2):
         for i in range(2, 4):
             gathers[way, 2, SUB_ORDER[way][i]].wait_recv()
-        for i in range(2):
-            gathers[way, 3, SUB_ORDER[way][i]].wait_recv()
-    for i in range(5):
-        multiply(5, 3, i)
+    for part_of in range(2):
+        for way in range(2):
+            gathers[way, 3, SUB_ORDER[way][part_of]].wait_recv()
+        for i in range(5):
+            multiply(5, 3, i, (part_of, part_of + 2), part_of > 0)
     summarize(5, 3)
 
     blocks = [stats[0:CH, :]]
@@ -474,9 +551,7 @@
     for block in blocks:
         mass = mass + block[:, 1:2] * jnp.exp(block[:, 0:1] - top)
         hit = hit + block[:, 2:3]
-    result = jnp.broadcast_to(hit - top - jnp.log(mass), (CH, HD))
-    padded = jnp.concatenate([result, jnp.zeros((HD - CH, HD), F32)], axis=0)
-    out_ref[...] = padded.T[0:1, 0:CH]
+    out_ref[...] = as_row(hit - top - jnp.log(mass))[0:1, 0:CH]
     for copy in waiting:
         copy.wait_send()
 
@@ -492,9 +567,17 @@
     result = pl.pallas_call(
         kernel,
         out_shape=jax.ShapeDtypeStruct((1, CH), F32),
-        in_specs=[vmem] * 8 + [hbm] * 2,
+        in_specs=[hbm] * 10,
         out_specs=vmem,
         scratch_shapes=[
+            pltpu.VMEM((TOK, 2 * HD), BF16),
+            pltpu.VMEM((TOK, 2 * HD), BF16),
+            pltpu.VMEM((TOK, 2 * HD), BF16),
+            pltpu.VMEM((2, TOK), F32),
+            pltpu.VMEM((1, TOK), jnp.int32),
+            pltpu.VMEM((1, TOK), jnp.int32),
+            pltpu.VMEM((CH, D), BF16),
+            pltpu.VMEM((1, D), F32),
             pltpu.VMEM((512, D), BF16),
             pltpu.VMEM((D, 2 * NV), BF16),
             pltpu.VMEM((NZ, CH, D), F32),
@@ -502,7 +585,7 @@
             pltpu.VMEM((2, 4, CH, D), BF16),
             pltpu.VMEM((NZ * CH, D), BF16),
             pltpu.VMEM((NZ * CH, 2 * NV), F32),
-            pltpu.VMEM((CH, D), F32),
+            pltpu.VMEM((NZ, 8, HD), F32),
             pltpu.VMEM((2, TOK, HD), F32),
             pltpu.VMEM((TOK, HD), F32),
             pltpu.VMEM((NZ * CH, HD), F32),
@@ -513,7 +596,7 @@
             pltpu.VMEM((5, 2 * HD + 16, HD), BF16),
             pltpu.VMEM((NZ * CH, HD), F32),
             pltpu.VMEM((NZ, CH, HD), F32),
-            dma((2,)),
+            dma((10,)),
             dma((pieces, 9)),
             dma((pieces, 9)),
             dma((5,)),
@@ -524,6 +607,8 @@
             dma((32,)),
             dma((32,)),
             dma((32,)),
+            dma((NZ,)),
+            dma((NZ,)),
             dma((NZ,)),
             dma((NZ,)),
         ],

time: 123 us -> 104 us (0.85)
  Pallas kernels: 120 us -> 102 us
    pallas_call x1, Pallas kernels: 120 us -> 102 us  [shards(): pl.pallas_call(kernel, out_shape=jax.ShapeDtypeStruct((1, CH), F32), in_s...]
where the time goes in v2:
time: 104 us; the launch traced here: 103 us
  Pallas kernels  102 us (98%)
  local copies, waits for them, and re-layouts  1.19 us (1%)
    pallas_call x1, Pallas kernels, shards(): pl.pallas_call(kernel, out_shape=jax.ShapeDtypeStruct((1, CH), F32), in_s...  102 us

profile of v2, /device:TPU:24, one launch (start us, length us, event | category | flops | bytes accessed | tf_op | source)
XLA Modules:
  0.0 102.9 jit_solution(10581883649554099175)
XLA Ops:
  0.0 101.7 %layer.1 = f32[1,32]{1,0:T(1,128)} custom-call(bf16[512,256]{1,0:T(8,128)(2,1)} %q_hbm.1, bf16[512,256]{1,0:T(8,128)(2,1)} %k_hbm.1, bf16[512,256]{1,0:T(8,128)(2,1)} %v_hbm.1, f32[2,512]{1,0:T(2,128)} %ld_hbm.1, s32[1,512]{1,0:T(1,128)} %bitcast.5, s32[1,512]{1,0:T(1,128)} %bitcast.6, bf16[32,6144]{1,0:T(8,128)(2,1)} %res_hbm.1, f32[1,6144]{1,0:T(1,128)} %bitcast.4, ...), custom_call_target="tpu_custom_call" | custom-call | tf_op jit(solution)/shard_map/layer/pallas_call | solution.py:567
  101.7 1.2 %copy.12 = f32[32]{0:T(128)} copy(f32[32]{0:T(128)} %bitcast.7) | data formatting | bytes 256

commit v3 on v1

v3 whole, which is shorter than its diff:
```python
import jax
import jax.numpy as jnp
from jax import lax
from jax.experimental import pallas as pl
from jax.experimental.pallas import tpu as pltpu
from jax.sharding import PartitionSpec as P

EPSILON = 1e-06
MESH = pl.DeviceIdType.MESH
F32 = jnp.float32
BF16 = jnp.bfloat16

TOK = 512
D = 6144
HD = 128
NV = 640
CH = 32
NZ = 8
HALF = 256
DZ = 768
TILE = 256
COPIES = 192

SLOT_OFFSET = (0, -1, 1, -2, 2, -3, 3, 4)
GATHER_FROM = ((0, 1, 3, 5), (0, 2, 4, 6))
GATHER_TO = ((1, 3, 5, 7), (2, 4, 6, 7))

KINDS = "XYYYYY"
WH_ROWS = 1024


def dot(a, b):
    return jnp.dot(a, b, preferred_element_type=F32)


def kernel(
    q_hbm, k_hbm, v_hbm, ld_hbm, seg_hbm, tgt_hbm, res_hbm, gain_hbm, wo_ref, wh_ref,
    out_ref,
    q_ref, k_ref, v_ref, ld_ref, seg_ref, tgt_ref, res, gain_ref,
    wo, wh, attn, heads, partial, swap_out, swap_in, slices, logits, squares, within, columns, goals,
    state_out, state_in, stats, stats_out, stats_in,
    local_sem, send_sem, recv_sem,
):
    ctx = lax.axis_index("ctx")
    vocab = lax.axis_index("vocab")
    x_lo = ctx // 8
    y = lax.rem(ctx // 2, 4)
    core = lax.rem(ctx, 2)
    z = vocab // 2
    x_hi = lax.rem(vocab, 2)

    def at_y(by):
        return x_lo * 8 + lax.rem(y + by + 4, 4) * 2 + core

    def along_z(by):
        return lax.rem(z + by + NZ, NZ)

    sibling = (ctx + 1 - 2 * core, vocab)
    y_peer = {by: (at_y(by), vocab) for by in (-1, 1, 2)}
    lo_peer = (lax.rem(ctx + 8, 16), vocab)
    cut_peer = (lax.rem(ctx + 8, 16), z * 2 + 1 - x_hi)
    hi_peer = (ctx, z * 2 + 1 - x_hi)
    z_peer = {by: (ctx, along_z(by) * 2 + x_hi) for by in (-3, -2, -1, 1, 2, 3, 4)}

    barrier = pltpu.get_barrier_semaphore()
    peers = [sibling, lo_peer, cut_peer, hi_peer, *y_peer.values(), *z_peer.values()]
    for peer in peers:
        pl.semaphore_signal(barrier, inc=1, device_id=peer, device_id_type=MESH)

    def load(index, src, dst):
        copy = pltpu.make_async_copy(src, dst, local_sem.at[index])
        copy.start()
        return copy

    small = [
        load(0, ld_hbm, ld_ref), load(1, seg_hbm, seg_ref), load(2, tgt_hbm, tgt_ref),
        load(3, k_hbm, k_ref), load(4, v_hbm, v_ref),
    ]
    load_q = load(5, q_hbm, q_ref)

    moves = {}

    def move(name, src, dst, peer):
        index = len(moves)
        copy = pltpu.make_async_remote_copy(
            src_ref=src, dst_ref=dst, send_sem=send_sem.at[index], recv_sem=recv_sem.at[index],
            device_id=peer, device_id_type=MESH,
        )
        copy.start()
        moves[name] = copy

    def arrived(*name):
        moves[name].wait_recv()

    def strip(at_lo, at_row, of_core):
        return of_core * 8 + at_lo * 4 + at_row

    def item(lo, by, first=0, count=NZ):
        row = lax.rem(y + by + 4, 4)
        return wo.at[pl.ds(first, count), strip(lax.rem(x_lo + lo, 2), row, core)]

    own_strip = strip(x_lo, y, core)

    def pass_item(name, lo, by, peer, first=0, count=NZ):
        view = item(lo, by, first, count)
        move(name, view, view, peer)

    def wo_0():
        rows = pl.ds(pl.multiple_of(own_strip * 16, 16), 16)
        for by in (1, -1, 2, -2, 3, -3, 4):
            cols = pl.ds(pl.multiple_of(along_z(by) * DZ, 128), DZ)
            move(("wz", by), wo_ref.at[rows, cols], wo.at[z, own_strip], z_peer[by])
        cols = pl.ds(pl.multiple_of(z * DZ, 128), DZ)
        return load(6, wo_ref.at[rows, cols], wo.at[z, own_strip])

    def to_core(lo, by):
        pass_item(("core", lo, by), lo, by, sibling)

    def wo_1():
        for by in (1, -1, 2, -2, 3, -3, 4):
            arrived("wz", by)
        own_strip_copy.wait()
        pass_item(("up", 0), 0, 0, y_peer[1])
        pass_item(("down", 0), 0, 0, y_peer[-1])
        pass_item(("lo", 0), 0, 0, lo_peer)
        to_core(0, 0)

    def wo_2():
        arrived("up", 0)
        pass_item(("up2", 0), 0, -1, y_peer[1], 0, 4)
        pass_item(("lo", -1), 0, -1, lo_peer, 0, 4)
        to_core(0, -1)
        arrived("down", 0)
        pass_item(("down2", 0), 0, 1, y_peer[-1], 4, 4)
        pass_item(("lo", 1), 0, 1, lo_peer, 0, 4)
        to_core(0, 1)

    def wo_3():
        arrived("lo", 0)
        pass_item(("up", 1), 1, 0, y_peer[1], 4, 4)
        pass_item(("down", 1), 1, 0, y_peer[-1], 4, 4)
        to_core(1, 0)

    def wo_4():
        arrived("up2", 0)
        arrived("down2", 0)
        pass_item(("lo", 2), 0, 2, lo_peer, 0, 4)
        to_core(0, 2)
        arrived("up", 1)
        pass_item(("up2", 1), 1, -1, y_peer[1], 4, 2)
        arrived("lo", -1)
        to_core(1, -1)
        arrived("down", 1)
        pass_item(("down2", 1), 1, 1, y_peer[-1], 6, 2)
        arrived("lo", 1)
        to_core(1, 1)

    def wo_5():
        arrived("up2", 1)
        arrived("down2", 1)
        arrived("lo", 2)
        to_core(1, 2)

    def wo_6():
        for lo in range(2):
            for by in (0, -1, 1, 2):
                arrived("core", lo, by)

    def part_rows(piece):
        return WH_ROWS // (8 if KINDS[piece] == "Y" else 4)

    def part_start(piece, by):
        if KINDS[piece] == "Y":
            index = lax.rem(y + by + 4, 4) * 2 + core
        else:
            index = lax.rem(x_lo + by, 2) * 2 + core
        return index * part_rows(piece) + piece * WH_ROWS

    def piece_view(piece, by, low=0, size=None):
        size = part_rows(piece) if size is None else size
        return wh.at[pl.ds(pl.multiple_of(part_start(piece, by) + low, 16), size), pl.ds(NV, NV)]

    def fetch_0(piece):
        by = 0 if KINDS[piece] == "Y" else 1
        rows = pl.ds(pl.multiple_of(part_start(piece, by), 16), part_rows(piece))
        move(("cut", piece), wh_ref.at[rows, :], piece_view(piece, by), cut_peer)

    def fetch_1(piece):
        arrived("cut", piece)
        view = piece_view(piece, 0)
        if KINDS[piece] == "Y":
            move(("wup", piece), view, view, y_peer[1])
            move(("wdown", piece), view, view, y_peer[-1])
        else:
            move(("wlo", piece), view, view, lo_peer)
        move(("core0", piece), view, view, sibling)

    def fetch_2(piece):
        if KINDS[piece] == "X":
            arrived("wlo", piece)
            view = piece_view(piece, 1)
            move(("core1", piece), view, view, sibling)
            return
        half = part_rows(piece) // 2
        arrived("wup", piece)
        view = piece_view(piece, -1, 0, half)
        move(("wup2", piece), view, view, y_peer[1])
        view = piece_view(piece, -1)
        move(("core1", piece), view, view, sibling)
        arrived("wdown", piece)
        view = piece_view(piece, 1, half, half)
        move(("wdown2", piece), view, view, y_peer[-1])
        view = piece_view(piece, 1)
        move(("core2", piece), view, view, sibling)

    def fetch_3(piece):
        arrived("wup2", piece)
        arrived("wdown2", piece)
        view = piece_view(piece, 2)
        move(("core3", piece), view, view, sibling)

    def fetch_4(piece):
        for name in ("core0", "core1", "core2", "core3"):
            if (name, piece) in moves:
                arrived(name, piece)

    for copy in small:
        copy.wait()

    lane = lax.broadcasted_iota(jnp.int32, (8, TOK), 1)
    running = jnp.concatenate([ld_ref[...], jnp.zeros((6, TOK), F32)], axis=0)
    shift = 1
    while shift < TOK:
        running = running + jnp.where(lane >= shift, pltpu.roll(running, shift, axis=1), 0.0)
        shift *= 2
    seg_row = seg_ref[...].astype(F32)
    table = jnp.concatenate(
        [running[0:2], seg_row, tgt_ref[...].astype(F32), jnp.zeros((124, TOK), F32)], axis=0
    )
    columns[...] = table.T
    seg_col = columns[:, 2:3]
    seg_last = seg_col[TOK - 1 : TOK, :]

    decay = []
    own_state = []
    for h in range(2):
        head = slice(h * HD, (h + 1) * HD)
        cum_col = columns[:, h : h + 1]
        last = cum_col[TOK - 1 : TOK, :]
        tail = jnp.where(seg_col == seg_last, jnp.exp(last - cum_col), 0.0)
        weighted = (k_ref[:, head].astype(F32) * tail).astype(BF16)
        summary = lax.dot_general(
            weighted, v_ref[:, head], (((0,), (0,)), ((), ())), preferred_element_type=F32
        )
        own_state.append(summary)
        decay.append(jnp.exp(last))

    def pack(slot, states, decays, seg):
        for h in range(2):
            state_out[slot, h * HD : (h + 1) * HD, :] = states[h].astype(BF16)
        row = lax.broadcasted_iota(jnp.int32, (16, HD), 0)
        tops = [d.astype(BF16).astype(F32) for d in decays]
        block = jnp.where(row == 0, tops[0], 0.0)
        block = jnp.where(row == 1, decays[0] - tops[0], block)
        block = jnp.where(row == 2, tops[1], block)
        block = jnp.where(row == 3, decays[1] - tops[1], block)
        block = jnp.where(row == 4, seg, block)
        state_out[slot, 2 * HD : 2 * HD + 16, :] = block.astype(BF16)

    def unpack(buffer, slot):
        states = [buffer[slot, h * HD : (h + 1) * HD, :].astype(F32) for h in range(2)]
        block = buffer[slot, 2 * HD : 2 * HD + 16, :].astype(F32)
        decays = [block[0:1, 0:1] + block[1:2, 0:1], block[2:3, 0:1] + block[3:4, 0:1]]
        return states, decays, block[4:5, 0:1]

    def join(first, second):
        states = [
            jnp.where(first[2] == second[2], second[1][h], 0.0) * first[0][h] + second[0][h]
            for h in range(2)
        ]
        return states, [first[1][h] * second[1][h] for h in range(2)], second[2]

    def choose(flag, a, b):
        return (
            [jnp.where(flag, a[0][h], b[0][h]) for h in range(2)],
            [jnp.where(flag, a[1][h], b[1][h]) for h in range(2)],
            jnp.where(flag, a[2], b[2]),
        )

    pack(0, own_state, decay, seg_last)
    pl.semaphore_wait(barrier, len(peers))
    move(("core",), state_out.at[0], state_in.at[0], sibling)
    own_strip_copy = wo_0()
    for by in (1, -1, 2, -2, 3, -3, 4):
        cols = pl.ds(pl.multiple_of(along_z(by) * DZ, 128), DZ)
        move(("res", by), res_hbm.at[:, cols], res.at[z], z_peer[by])
    cols = pl.ds(pl.multiple_of(z * DZ, 128), DZ)
    own_res = load(7, res_hbm.at[:, cols], res.at[z])
    load_gain = load(8, gain_hbm.at[:, cols], gain_ref)
    for piece in range(len(KINDS)):
        fetch_0(piece)
    own_wh = load(9, wh_ref, wh.at[:, pl.ds(0, NV)])

    def inside(h):
        head = slice(h * HD, (h + 1) * HD)
        cum_col = columns[:, h : h + 1]
        cum_row = running[h : h + 1, :]
        for low in (0, 256):
            high = low + 256
            scores = lax.dot_general(
                q_ref[low:high, head], k_ref[0:high, head], (((1,), (1,)), ((), ())),
                preferred_element_type=F32,
            )
            at_row = lax.broadcasted_iota(jnp.int32, (256, high), 0) + low
            at_col = lax.broadcasted_iota(jnp.int32, (256, high), 1)
            allowed = (at_row >= at_col) & (seg_col[low:high] == seg_row[:, 0:high])
            spread = cum_col[low:high] - cum_row[:, 0:high]
            weights = jnp.exp(jnp.where(allowed, spread, -1e30))
            mixing = (scores * weights).astype(BF16)
            within[h, low:high, :] = dot(mixing, v_ref[0:high, head])

    arrived("core")

    own = (own_state, decay, seg_last)
    other = unpack(state_in, 0)
    first = choose(core == 0, own, other)
    second = choose(core == 0, other, own)
    chip = join(first, second)
    pack(1, *chip)
    for index, by in enumerate((-1, 1, 2)):
        move(("state", by), state_out.at[1], state_in.at[1 + index], y_peer[by])
    load_q.wait()
    inside(0)
    inside(1)
    for by in (-1, 1, 2):
        arrived("state", by)
    chips = {0: chip}
    for index, by in enumerate((1, -1, 2)):
        chips[by] = unpack(state_in, 1 + index)

    def chip_at(target):
        picked = chips[0]
        for by in (1, -1, 2):
            picked = choose(lax.rem(y + by + 4, 4) == target, chips[by], picked)
        return picked

    nothing = ([jnp.zeros((HD, HD), F32)] * 2, [jnp.ones((1, 1), F32)] * 2, jnp.zeros((1, 1), F32))
    total = chip_at(0)
    before = choose(y == 0, nothing, total)
    for target in range(1, 4):
        total = join(total, chip_at(target))
        before = choose(y > target, total, before)
    pack(2, *total)
    move(("total",), state_out.at[2], state_in.at[4], lo_peer)
    wo_1()
    arrived("total")
    earlier = unpack(state_in, 4)
    joined = choose(y == 0, earlier, join(earlier, before))
    before = choose(x_lo == 0, before, joined)
    fresh = (x_lo == 0) & (y == 0)
    with_first = choose(fresh, first, join(before, first))
    before = choose(core == 0, before, with_first)
    prior = before[2]


    def own_heads(sub):
        return attn.at[sub % 2, 1 - x_hi if sub < 2 else x_hi]

    def gather_heads(way, step, sub):
        if step > 0:
            arrived("heads", way, step - 1, sub)
        src = own_heads(sub) if step == 0 else heads.at[GATHER_FROM[way][step], sub]
        dst = heads.at[GATHER_TO[way][step], sub]
        move(("heads", way, step, sub), src, dst, z_peer[1 if way == 0 else -1])

    for h in range(2):
        head = slice(h * HD, (h + 1) * HD)
        scale = jnp.where(seg_col == prior, jnp.exp(columns[:, h : h + 1]), 0.0)
        carried = dot(q_ref[:, head], before[0][h].astype(BF16))
        output = within[h] + scale * carried
        mean = jnp.mean(output * output, axis=-1, keepdims=True)
        scaled = (output * lax.rsqrt(mean + EPSILON)).astype(BF16)
        for j in range(NZ):
            for half in range(2):
                low = (2 * j + half) * CH
                attn[h, half, j * CH : (j + 1) * CH] = scaled[low : low + CH]
    for sub in range(4):
        for way in range(2):
            gather_heads(way, 0, sub)
    wo_2()
    wo_3()
    for j in range(NZ):
        rows = pl.ds(pl.multiple_of((2 * j + x_hi) * CH, CH), CH)
        goals[j * CH : (j + 1) * CH, :] = columns[rows, :]
    for sub in range(2):
        for way in range(2):
            gather_heads(way, 1, sub)
    wo_4()
    for sub in range(2, 4):
        for way in range(2):
            gather_heads(way, 1, sub)
    wo_5()
    fetch_1(0)
    for sub in range(4):
        for way in range(2):
            gather_heads(way, 2, sub)
        if sub == 0:
            fetch_1(1)
            fetch_1(2)
        if sub == 2:
            fetch_1(3)
            fetch_1(4)
    wo_6()

    def project(slot, near):
        if slot == 0:
            left = jnp.concatenate([own_heads(2 * near + h)[...] for h in range(2)], axis=1)
        else:
            left = jnp.concatenate([heads[slot, 2 * near + h] for h in range(2)], axis=1)
        return dot(left, wo[along_z(SLOT_OFFSET[slot])].reshape(HALF, DZ))

    for near in range(2):
        partial[near] = project(0, near) + project(1, near) + project(2, near)
    for sub in (0, 2):
        gather_heads(0, 3, sub)
        gather_heads(1, 3, sub + 1)
    fetch_1(5)
    for near in range(2):
        partial[near] += project(3, near) + project(4, near)
    own_res.wait()
    load_gain.wait()
    for by in (1, -1, 2, -2, 3, -3, 4):
        arrived("res", by)
    partial[1] += res[...].reshape(HALF, DZ).astype(F32)
    for sub in (0, 2):
        arrived("heads", 1, 2, sub)
        arrived("heads", 0, 2, sub + 1)
    for near in range(2):
        partial[near] += project(5, near) + project(6, near)
    arrived("heads", 0, 3, 0)
    arrived("heads", 1, 3, 1)
    far = partial[0] + project(7, 0)
    for sub in range(4):
        rows = slice(sub * 64, (sub + 1) * 64)
        swap_out[rows, :] = far[rows].astype(BF16)
        view = pl.ds(sub * 64, 64)
        move(("swap", sub), swap_out.at[view], swap_in.at[view], hi_peer)
    arrived("heads", 0, 3, 2)
    arrived("heads", 1, 3, 3)
    partial[1] += project(7, 1)

    def sub_rows(sub):
        return pl.ds(sub * 64, 64)

    def gather_hidden(way, step, sub):
        if step > 0:
            arrived("hidden", way, step - 1, sub)
        src = slices.at[GATHER_FROM[way][step], sub_rows(sub)]
        dst = slices.at[GATHER_TO[way][step], sub_rows(sub)]
        move(("hidden", way, step, sub), src, dst, z_peer[1 if way == 0 else -1])

    order = ((0, 2, 1, 3), (1, 3, 0, 2))
    for sub in range(4):
        arrived("swap", sub)
        rows = slice(sub * 64, (sub + 1) * 64)
        value = partial[1, rows, :] + swap_in[rows, :].astype(F32)
        partial[1, rows, :] = value
        slices[0, rows, :] = (value * gain_ref[...]).astype(BF16)
        for way in range(2):
            gather_hidden(way, 0, sub)
    square = jnp.sum(partial[1] * partial[1], axis=1, keepdims=True)
    turned = jnp.broadcast_to(square, (HALF, HD)).T
    squares[0] = jnp.concatenate(
        [turned[0:1, 0:HD], turned[0:1, HD:HALF], jnp.zeros((6, HD), F32)], axis=0
    )
    for slot in range(1, NZ):
        offset = SLOT_OFFSET[slot]
        peer = z_peer[offset if slot == NZ - 1 else -offset]
        move(("square", slot), squares.at[0], squares.at[slot], peer)

    own_offset = vocab * NV
    other_offset = (z * 2 + 1 - x_hi) * NV

    def multiply(slots, low, high, cols, more=True):
        value = logits[low:high, cols] if more else 0.0
        for slot in slots:
            deep = pl.ds(pl.multiple_of(along_z(SLOT_OFFSET[slot]) * DZ, DZ), DZ)
            value = value + dot(slices[slot, low:high, :], wh[deep, cols])
        logits[low:high, cols] = value

    def summarize(low, high):
        size = high - low
        values = logits[low:high, :] * factor[low:high]
        top = jnp.max(values, axis=1, keepdims=True)
        mass = jnp.sum(jnp.exp(values - top), axis=1, keepdims=True)
        column = lax.broadcasted_iota(jnp.int32, (size, 2 * NV), 1)
        column = jnp.where(column < NV, column + own_offset, column - NV + other_offset)
        goal = goals[low:high, 3:4].astype(jnp.int32)
        hit = jnp.sum(jnp.where(column == goal, values, 0.0), axis=1, keepdims=True)
        lane_of = lax.broadcasted_iota(jnp.int32, (size, HD), 1)
        stats[low:high, :] = jnp.where(lane_of == 0, top, jnp.where(lane_of == 1, mass, hit))

    own_tiles = (slice(0, 256), slice(256, 512), slice(512, 640))
    other_tiles = (slice(640, 896), slice(896, 1152), slice(1152, 1280))
    all_tiles = tuple(slice(i * TILE, (i + 1) * TILE) for i in range(5))
    own_wh.wait()
    fetch_2(0)
    service = {
        (1, 0): [(fetch_2, 1), (fetch_2, 2)],
        (1, 1): [(fetch_2, 3)],
        (1, 2): [(fetch_2, 4)],
        (1, 3): [(fetch_2, 5)],
        (2, 0): [(fetch_3, 1)],
        (2, 1): [(fetch_3, 2)],
        (2, 2): [(fetch_3, 3), (fetch_3, 4)],
        (2, 3): [(fetch_3, 5)],
    }
    for step in (1, 2):
        for i in range(4):
            for way in range(2):
                gather_hidden(way, step, order[way][i])
            for fetch, piece in service.get((step, i), ()):
                fetch(piece)
    for i in range(2):
        for way in range(2):
            gather_hidden(way, 3, order[way][i])
    for tile in own_tiles:
        multiply((0, 1, 2, 3, 4), 0, HALF, tile, False)
    for piece in range(len(KINDS)):
        fetch_4(piece)
    for tile in other_tiles:
        multiply((0, 1, 2, 3, 4), 0, HALF, tile, False)
    total_square = squares[0]
    for slot in range(1, NZ):
        arrived("square", slot)
        total_square = total_square + squares[slot]
    factor = lax.rsqrt(total_square / D + EPSILON)
    factor = jnp.concatenate([factor, jnp.zeros((HD - 8, HD), F32)], axis=0).T
    factor = jnp.concatenate([factor[:, 0:1], factor[:, 1:2]], axis=0)
    for way in range(2):
        for i in range(2, 4):
            arrived("hidden", way, 2, order[way][i])
    for tile in all_tiles:
        multiply((5, 6), 0, HALF, tile)
    for i in range(2):
        for way in range(2):
            arrived("hidden", way, 3, order[way][i])
        for tile in all_tiles:
            multiply((7,), i * 128, i * 128 + 128, tile)
        summarize(i * 128, i * 128 + 128)
    turned = stats[...].T
    for half in range(2):
        stats_out[half] = turned[0:8, half * HD : (half + 1) * HD]
    for by in (4, 3, -3, 2, -2, 1, -1):
        move(("stats", by), stats_out.at[along_z(by) // 4], stats_in.at[by + 3], z_peer[by])
    blocks = [stats_out[z // 4]]
    for by in (1, -1, 2, -2, 3, -3, 4):
        arrived("stats", by)
        blocks.append(stats_in[by + 3])
    top = blocks[0][0:1]
    for block in blocks[1:]:
        top = jnp.maximum(top, block[0:1])
    mass = jnp.zeros((1, HD), F32)
    hit = jnp.zeros((1, HD), F32)
    for block in blocks:
        mass = mass + block[1:2] * jnp.exp(block[0:1] - top)
        hit = hit + block[2:3]
    result = hit - top - jnp.log(mass)
    quarter = lax.rem(z, 4)
    picked = result[:, 0:CH]
    for i in range(1, 4):
        picked = jnp.where(quarter == i, result[:, i * CH : (i + 1) * CH], picked)
    out_ref[...] = picked
    for copy in moves.values():
        copy.wait_send()


def shards(
    query_rows, key_rows, value_rows, log_decay, segment_ids, residual, out_weight, final_gain,
    head_weight, targets,
):
    vmem = pl.BlockSpec(memory_space=pltpu.VMEM)
    hbm = pl.BlockSpec(memory_space=pl.ANY)
    dma = pltpu.SemaphoreType.DMA
    result = pl.pallas_call(
        kernel,
        out_shape=jax.ShapeDtypeStruct((1, CH), F32),
        in_specs=[hbm] * 10,
        out_specs=vmem,
        scratch_shapes=[
            pltpu.VMEM((TOK, 2 * HD), BF16),
            pltpu.VMEM((TOK, 2 * HD), BF16),
            pltpu.VMEM((TOK, 2 * HD), BF16),
            pltpu.VMEM((2, TOK), F32),
            pltpu.VMEM((1, TOK), jnp.int32),
            pltpu.VMEM((1, TOK), jnp.int32),
            pltpu.VMEM((NZ, CH, DZ), BF16),
            pltpu.VMEM((1, DZ), F32),
            pltpu.VMEM((NZ, 16, 16, DZ), BF16),
            pltpu.VMEM((D, 2 * NV), BF16),
            pltpu.VMEM((2, 2, HALF, HD), BF16),
            pltpu.VMEM((NZ, 4, HALF, HD), BF16),
            pltpu.VMEM((2, HALF, DZ), F32),
            pltpu.VMEM((HALF, DZ), BF16),
            pltpu.VMEM((HALF, DZ), BF16),
            pltpu.VMEM((NZ, HALF, DZ), BF16),
            pltpu.VMEM((HALF, 2 * NV), F32),
            pltpu.VMEM((NZ, 8, HD), F32),
            pltpu.VMEM((2, TOK, HD), F32),
            pltpu.VMEM((TOK, HD), F32),
            pltpu.VMEM((HALF, HD), F32),
            pltpu.VMEM((3, 2 * HD + 16, HD), BF16),
            pltpu.VMEM((5, 2 * HD + 16, HD), BF16),
            pltpu.VMEM((HALF, HD), F32),
            pltpu.VMEM((2, 8, HD), F32),
            pltpu.VMEM((NZ, 8, HD), F32),
            dma((10,)),
            dma((COPIES,)),
            dma((COPIES,)),
        ],
        compiler_params=pltpu.CompilerParams(
            collective_id=0, has_side_effects=True, vmem_limit_bytes=56 * 1024 * 1024
        ),
        name="layer",
    )(
        query_rows, key_rows, value_rows, log_decay, segment_ids.reshape(1, -1),
        targets.reshape(1, -1), residual, final_gain.reshape(1, -1), out_weight, head_weight,
    )
    return result.reshape(CH)


def solution(mesh):
    in_specs = (
        P("ctx", "vocab"),
        P("ctx", "vocab"),
        P("ctx", "vocab"),
        P("vocab", "ctx"),
        P("ctx"),
        P(("ctx", "vocab"), None),
        P("vocab", None),
        P(),
        P(None, "vocab"),
        P("ctx"),
    )
    out_specs = P(("ctx", "vocab"))
    return jax.shard_map(shards, mesh=mesh, in_specs=in_specs, out_specs=out_specs, check_vma=False)
```

time: 123 us -> 90.4 us (0.73); the launches traced: 121 us -> 89.8 us
  Pallas kernels: 120 us -> 88.6 us
    pallas_call x1, Pallas kernels: 120 us -> 88.6 us  [shards(): pl.pallas_call(kernel, out_shape=jax.ShapeDtypeStruct((1, CH), F32), in_s...]
where the time goes in v3:
time: 90.4 us; the launch traced here: 89.8 us
  Pallas kernels  88.6 us (98%)
  local copies, waits for them, and re-layouts  1.19 us (1%)
    pallas_call x1, Pallas kernels, shards(): pl.pallas_call(kernel, out_shape=jax.ShapeDtypeStruct((1, CH), F32), in_s...  88.6 us

profile of v3, /device:TPU:24, one launch (start us, length us, event | category | flops | bytes accessed | tf_op | source)
XLA Modules:
  0.0 89.8 jit_solution(4776403885943566681)
XLA Ops:
  0.0 88.6 %layer.1 = f32[1,32]{1,0:T(1,128)} custom-call(bf16[512,256]{1,0:T(8,128)(2,1)} %q_hbm.1, bf16[512,256]{1,0:T(8,128)(2,1)} %k_hbm.1, bf16[512,256]{1,0:T(8,128)(2,1)} %v_hbm.1, f32[2,512]{1,0:T(2,128)} %ld_hbm.1, s32[1,512]{1,0:T(1,128)} %bitcast.5, s32[1,512]{1,0:T(1,128)} %bitcast.6, bf16[32,6144]{1,0:T(8,128)(2,1)} %res_hbm.1, f32[1,6144]{1,0:T(1,128)} %bitcast.4, ...), custom_call_target="tpu_custom_call" | custom-call | tf_op jit(solution)/shard_map/layer/pallas_call | solution.py:585
  88.7 1.2 %copy.12 = f32[32]{0:T(128)} copy(f32[32]{0:T(128)} %bitcast.7) | data formatting | bytes 256

commit v4 on v3

v4 whole, which is shorter than its diff:
```python
import jax
import jax.numpy as jnp
from jax import lax
from jax.experimental import pallas as pl
from jax.experimental.pallas import tpu as pltpu
from jax.sharding import PartitionSpec as P

EPSILON = 1e-06
MESH = pl.DeviceIdType.MESH
F32 = jnp.float32
BF16 = jnp.bfloat16

TOK = 512
D = 6144
HD = 128
NV = 640
CH = 32
NZ = 8
HALF = 256
DZ = 768
TILE = 256
ARRIVALS = 65
GROUPS = ("state", "res", "strip", "wo", "wh", "heads", "swap", "hidden", "square", "stats")

OTHERS = (1, -1, 2, -2, 3, -3, 4)
SLOT_OFFSET = (0, -1, 1, -2, 2, -3, 3, 4)
GATHER_FROM = ((0, 1, 3, 5), (0, 2, 4, 6))
GATHER_TO = ((1, 3, 5, 7), (2, 4, 6, 7))

KINDS = "XYYYYY"
WH_ROWS = 1024


def dot(a, b):
    return jnp.dot(a, b, preferred_element_type=F32)


def kernel(
    q_hbm, k_hbm, v_hbm, ld_hbm, seg_hbm, tgt_hbm, res_hbm, gain_hbm, wo_ref, wh_ref,
    out_ref,
    q_ref, k_ref, v_ref, ld_ref, seg_ref, tgt_ref, res, gain_ref,
    wo, wh, attn, heads, partial, hidden, swap_out, swap_in, slices, logits, squares, within, columns, goals,
    state_out, state_in, stats, stats_out, stats_in,
    local_sem, send_sem, recv_sem,
):
    ctx = lax.axis_index("ctx")
    vocab = lax.axis_index("vocab")
    x_lo = ctx // 8
    y = lax.rem(ctx // 2, 4)
    core = lax.rem(ctx, 2)
    z = vocab // 2
    x_hi = lax.rem(vocab, 2)

    def at_y(by):
        return x_lo * 8 + lax.rem(y + by + 4, 4) * 2 + core

    def along_z(by):
        return lax.rem(z + by + NZ, NZ)

    sibling = (ctx + 1 - 2 * core, vocab)
    y_peer = {by: (at_y(by), vocab) for by in (-1, 1, 2)}
    lo_peer = (lax.rem(ctx + 8, 16), vocab)
    cut_peer = (lax.rem(ctx + 8, 16), z * 2 + 1 - x_hi)
    hi_peer = (ctx, z * 2 + 1 - x_hi)
    z_peer = {by: (ctx, along_z(by) * 2 + x_hi) for by in (-3, -2, -1, 1, 2, 3, 4)}

    barrier = pltpu.get_barrier_semaphore()
    peers = [sibling, lo_peer, cut_peer, hi_peer, *y_peer.values(), *z_peer.values()]
    for peer in peers:
        pl.semaphore_signal(barrier, inc=1, device_id=peer, device_id_type=MESH)

    def load(index, src, dst):
        copy = pltpu.make_async_copy(src, dst, local_sem.at[index])
        copy.start()
        return copy

    small = [
        load(0, ld_hbm, ld_ref), load(1, seg_hbm, seg_ref), load(2, tgt_hbm, tgt_ref),
        load(3, k_hbm, k_ref), load(4, v_hbm, v_ref),
    ]
    load_q = load(5, q_hbm, q_ref)

    arrivals = {}

    def move(group, key, src, dst, peer):
        index = arrivals.setdefault(key, len(arrivals))
        pltpu.make_async_remote_copy(
            src_ref=src, dst_ref=dst, send_sem=send_sem.at[GROUPS.index(group)],
            recv_sem=recv_sem.at[index], device_id=peer, device_id_type=MESH,
        ).start()

    def arrived(like, *key):
        pltpu.make_async_copy(like, like, recv_sem.at[arrivals[key]]).wait()

    def departed(like, group):
        pltpu.make_async_copy(like, like, send_sem.at[GROUPS.index(group)]).wait()

    def strip(at_lo, at_row, of_core):
        return of_core * 8 + at_lo * 4 + at_row

    def item(lo, by, first=0, count=NZ):
        row = lax.rem(y + by + 4, 4)
        return wo.at[pl.ds(first, count), strip(lax.rem(x_lo + lo, 2), row, core)]

    own_strip = strip(x_lo, y, core)

    def pass_item(key, lo, by, peer, first=0, count=NZ):
        view = item(lo, by, first, count)
        move("wo", key, view, view, peer)

    def wo_0():
        rows = pl.ds(pl.multiple_of(own_strip * 16, 16), 16)
        for by in OTHERS:
            cols = pl.ds(pl.multiple_of(along_z(by) * DZ, 128), DZ)
            move("strip", ("z",), wo_ref.at[rows, cols], wo.at[z, own_strip], z_peer[by])
        cols = pl.ds(pl.multiple_of(z * DZ, 128), DZ)
        return load(6, wo_ref.at[rows, cols], wo.at[z, own_strip])

    one_item = wo.at[0, pl.ds(0, 8)]

    def to_core(lo, by):
        view = item(lo, by)
        move("strip" if (lo, by) == (0, 0) else "wo", ("core",), view, view, sibling)

    def wo_1():
        arrived(wo.at[0, pl.ds(0, NZ - 1)], "z")
        own_strip_copy.wait()
        pass_item(("up",), 0, 0, y_peer[1])
        pass_item(("down",), 0, 0, y_peer[-1])
        pass_item(("lo",), 0, 0, lo_peer)
        to_core(0, 0)

    def wo_2():
        arrived(one_item, "up")
        pass_item(("far",), 0, -1, y_peer[1], 0, 4)
        pass_item(("lo_up",), 0, -1, lo_peer, 0, 4)
        to_core(0, -1)
        arrived(one_item, "down")
        pass_item(("far",), 0, 1, y_peer[-1], 4, 4)
        pass_item(("lo_down",), 0, 1, lo_peer, 0, 4)
        to_core(0, 1)

    def wo_3():
        arrived(one_item, "lo")
        pass_item(("lo_up",), 1, 0, y_peer[1], 4, 4)
        pass_item(("lo_down",), 1, 0, y_peer[-1], 4, 4)
        to_core(1, 0)

    def wo_4():
        arrived(one_item, "far")
        pass_item(("lo_far",), 0, 2, lo_peer, 0, 4)
        to_core(0, 2)
        arrived(one_item, "lo_up")
        pass_item(("lo_far",), 1, -1, y_peer[1], 4, 2)
        to_core(1, -1)
        arrived(one_item, "lo_down")
        pass_item(("lo_far",), 1, 1, y_peer[-1], 6, 2)
        to_core(1, 1)

    def wo_5():
        arrived(one_item, "lo_far")
        to_core(1, 2)

    def wo_6():
        arrived(wo.at[pl.ds(0, 4)], "core")

    def part_rows(piece):
        return WH_ROWS // (8 if KINDS[piece] == "Y" else 4)

    def part_start(piece, by):
        if KINDS[piece] == "Y":
            index = lax.rem(y + by + 4, 4) * 2 + core
        else:
            index = lax.rem(x_lo + by, 2) * 2 + core
        return index * part_rows(piece) + piece * WH_ROWS

    def piece_view(piece, by, low=0, size=None):
        size = part_rows(piece) if size is None else size
        return wh.at[pl.ds(pl.multiple_of(part_start(piece, by) + low, 16), size), pl.ds(NV, NV)]

    def wh_rows(count):
        return wh.at[pl.ds(0, count), pl.ds(0, NV)]

    def fetch_0(piece):
        by = 0 if KINDS[piece] == "Y" else 1
        rows = pl.ds(pl.multiple_of(part_start(piece, by), 16), part_rows(piece))
        move("wh", ("cut", piece), wh_ref.at[rows, :], piece_view(piece, by), cut_peer)

    def pass_part(key, view, peer):
        move("wh", key, view, view, peer)

    def fetch_1(piece):
        arrived(wh_rows(part_rows(piece)), "cut", piece)
        view = piece_view(piece, 0)
        if KINDS[piece] == "Y":
            pass_part(("next", piece), view, y_peer[1])
            pass_part(("next", piece), view, y_peer[-1])
        else:
            pass_part(("next", piece), view, lo_peer)
        pass_part(("wh_core",), view, sibling)

    def fetch_2(piece):
        size = part_rows(piece)
        if KINDS[piece] == "X":
            arrived(wh_rows(size), "next", piece)
            pass_part(("wh_core",), piece_view(piece, 1), sibling)
            return
        half = size // 2
        arrived(wh_rows(2 * size), "next", piece)
        pass_part(("second", piece), piece_view(piece, -1, 0, half), y_peer[1])
        pass_part(("second", piece), piece_view(piece, 1, half, half), y_peer[-1])
        pass_part(("wh_core",), piece_view(piece, -1), sibling)
        pass_part(("wh_core",), piece_view(piece, 1), sibling)

    def fetch_3(piece):
        arrived(wh_rows(part_rows(piece)), "second", piece)
        pass_part(("wh_core",), piece_view(piece, 2), sibling)

    def fetch_4():
        arrived(wh_rows(WH_ROWS // 2 * len(KINDS)), "wh_core")

    for copy in small:
        copy.wait()

    lane = lax.broadcasted_iota(jnp.int32, (8, TOK), 1)
    running = jnp.concatenate([ld_ref[...], jnp.zeros((6, TOK), F32)], axis=0)
    shift = 1
    while shift < TOK:
        running = running + jnp.where(lane >= shift, pltpu.roll(running, shift, axis=1), 0.0)
        shift *= 2
    seg_row = seg_ref[...].astype(F32)
    table = jnp.concatenate(
        [running[0:2], seg_row, tgt_ref[...].astype(F32), jnp.zeros((124, TOK), F32)], axis=0
    )
    columns[...] = table.T
    seg_col = columns[:, 2:3]
    seg_last = seg_col[TOK - 1 : TOK, :]

    decay = []
    own_state = []
    for h in range(2):
        head = slice(h * HD, (h + 1) * HD)
        cum_col = columns[:, h : h + 1]
        last = cum_col[TOK - 1 : TOK, :]
        tail = jnp.where(seg_col == seg_last, jnp.exp(last - cum_col), 0.0)
        weighted = (k_ref[:, head].astype(F32) * tail).astype(BF16)
        summary = lax.dot_general(
            weighted, v_ref[:, head], (((0,), (0,)), ((), ())), preferred_element_type=F32
        )
        own_state.append(summary)
        decay.append(jnp.exp(last))

    def pack(slot, states, decays, seg):
        for h in range(2):
            state_out[slot, h * HD : (h + 1) * HD, :] = states[h].astype(BF16)
        row = lax.broadcasted_iota(jnp.int32, (16, HD), 0)
        tops = [d.astype(BF16).astype(F32) for d in decays]
        block = jnp.where(row == 0, tops[0], 0.0)
        block = jnp.where(row == 1, decays[0] - tops[0], block)
        block = jnp.where(row == 2, tops[1], block)
        block = jnp.where(row == 3, decays[1] - tops[1], block)
        block = jnp.where(row == 4, seg, block)
        state_out[slot, 2 * HD : 2 * HD + 16, :] = block.astype(BF16)

    def unpack(buffer, slot):
        states = [buffer[slot, h * HD : (h + 1) * HD, :].astype(F32) for h in range(2)]
        block = buffer[slot, 2 * HD : 2 * HD + 16, :].astype(F32)
        decays = [block[0:1, 0:1] + block[1:2, 0:1], block[2:3, 0:1] + block[3:4, 0:1]]
        return states, decays, block[4:5, 0:1]

    def join(first, second):
        states = [
            jnp.where(first[2] == second[2], second[1][h], 0.0) * first[0][h] + second[0][h]
            for h in range(2)
        ]
        return states, [first[1][h] * second[1][h] for h in range(2)], second[2]

    def choose(flag, a, b):
        return (
            [jnp.where(flag, a[0][h], b[0][h]) for h in range(2)],
            [jnp.where(flag, a[1][h], b[1][h]) for h in range(2)],
            jnp.where(flag, a[2], b[2]),
        )

    pack(0, own_state, decay, seg_last)
    pl.semaphore_wait(barrier, len(peers))
    move("state", ("state_core",), state_out.at[0], state_in.at[0], sibling)
    own_strip_copy = wo_0()
    for by in OTHERS:
        cols = pl.ds(pl.multiple_of(along_z(by) * DZ, 128), DZ)
        move("res", ("res",), res_hbm.at[:, cols], res.at[z], z_peer[by])
    for piece in range(len(KINDS)):
        fetch_0(piece)
    cols = pl.ds(pl.multiple_of(z * DZ, 128), DZ)
    own_res = load(7, res_hbm.at[:, cols], res.at[z])
    load_gain = load(8, gain_hbm.at[:, cols], gain_ref)

    def inside(h):
        head = slice(h * HD, (h + 1) * HD)
        cum_col = columns[:, h : h + 1]
        cum_row = running[h : h + 1, :]
        for low in (0, 256):
            high = low + 256
            scores = lax.dot_general(
                q_ref[low:high, head], k_ref[0:high, head], (((1,), (1,)), ((), ())),
                preferred_element_type=F32,
            )
            at_row = lax.broadcasted_iota(jnp.int32, (256, high), 0) + low
            at_col = lax.broadcasted_iota(jnp.int32, (256, high), 1)
            allowed = (at_row >= at_col) & (seg_col[low:high] == seg_row[:, 0:high])
            spread = cum_col[low:high] - cum_row[:, 0:high]
            weights = jnp.exp(jnp.where(allowed, spread, -1e30))
            mixing = (scores * weights).astype(BF16)
            within[h, low:high, :] = dot(mixing, v_ref[0:high, head])

    arrived(state_in.at[0], "state_core")
    own_wh = load(9, wh_ref, wh.at[:, pl.ds(0, NV)])

    own = (own_state, decay, seg_last)
    other = unpack(state_in, 0)
    first = choose(core == 0, own, other)
    second = choose(core == 0, other, own)
    chip = join(first, second)
    pack(1, *chip)
    for index, by in enumerate((-1, 1, 2)):
        move("state", ("state_y",), state_out.at[1], state_in.at[1 + index], y_peer[by])
    load_q.wait()
    inside(0)
    inside(1)
    arrived(state_in.at[pl.ds(1, 3)], "state_y")
    chips = {0: chip}
    for index, by in enumerate((1, -1, 2)):
        chips[by] = unpack(state_in, 1 + index)

    def chip_at(target):
        picked = chips[0]
        for by in (1, -1, 2):
            picked = choose(lax.rem(y + by + 4, 4) == target, chips[by], picked)
        return picked

    nothing = ([jnp.zeros((HD, HD), F32)] * 2, [jnp.ones((1, 1), F32)] * 2, jnp.zeros((1, 1), F32))
    total = chip_at(0)
    before = choose(y == 0, nothing, total)
    for target in range(1, 4):
        total = join(total, chip_at(target))
        before = choose(y > target, total, before)
    pack(2, *total)
    move("state", ("total",), state_out.at[2], state_in.at[4], lo_peer)
    wo_1()
    arrived(state_in.at[4], "total")
    earlier = unpack(state_in, 4)
    joined = choose(y == 0, earlier, join(earlier, before))
    before = choose(x_lo == 0, before, joined)
    fresh = (x_lo == 0) & (y == 0)
    with_first = choose(fresh, first, join(before, first))
    before = choose(core == 0, before, with_first)
    prior = before[2]


    def own_heads(sub):
        return attn.at[x_hi if sub % 2 else 1 - x_hi, pl.ds(sub // 2 * 128, 128)]

    def wait_heads(step, key):
        arrived(heads.at[0, pl.ds(0, 2)], "heads", step, key)

    def send_heads(way, step, sub, key):
        src = own_heads(sub) if step == 0 else heads.at[GATHER_FROM[way][step], sub]
        dst = heads.at[GATHER_TO[way][step], sub]
        move("heads", ("heads", step, key), src, dst, z_peer[1 if way == 0 else -1])

    def gather_heads(step, sub):
        if step > 0:
            wait_heads(step - 1, sub)
        for way in range(2):
            send_heads(way, step, sub, sub)

    def last_heads(wave):
        for way in range(2):
            wait_heads(2, 2 * wave + way)
            send_heads(way, 3, 2 * wave + way, wave)

    for h in range(2):
        head = slice(h * HD, (h + 1) * HD)
        scale = jnp.where(seg_col == prior, jnp.exp(columns[:, h : h + 1]), 0.0)
        carried = dot(q_ref[:, head], before[0][h].astype(BF16))
        output = within[h] + scale * carried
        mean = jnp.mean(output * output, axis=-1, keepdims=True)
        scaled = (output * lax.rsqrt(mean + EPSILON)).astype(BF16)
        for j in range(NZ):
            for half in range(2):
                low = (2 * j + half) * CH
                attn[half, j * CH : (j + 1) * CH, head] = scaled[low : low + CH]
    for sub in range(3):
        gather_heads(0, sub)
    wo_2()
    wo_3()
    for j in range(NZ):
        rows = pl.ds(pl.multiple_of((2 * j + x_hi) * CH, CH), CH)
        goals[j * CH : (j + 1) * CH, :] = columns[rows, :]
    gather_heads(1, 0)
    gather_heads(1, 1)
    gather_heads(0, 3)
    gather_heads(2, 0)
    gather_heads(2, 1)
    wo_4()
    gather_heads(1, 2)
    fetch_1(0)
    wo_5()
    last_heads(0)
    gather_heads(1, 3)
    fetch_1(1)
    fetch_1(2)
    gather_heads(2, 2)
    wo_6()

    def project(slot, wave):
        if slot == 0:
            left = jnp.concatenate([own_heads(2 * wave + i)[...] for i in range(2)], axis=0)
        else:
            left = heads[slot, 2 * wave : 2 * wave + 2].reshape(HALF, HALF)
        return dot(left, wo[along_z(SLOT_OFFSET[slot])].reshape(HALF, DZ))

    def accumulate(wave, *slots):
        value = partial[wave]
        for slot in slots:
            value = value + project(slot, wave)
        partial[wave] = value

    def swap(wave):
        total = partial[wave] + project(7, wave)
        for i in range(2):
            sub = 2 * wave + i
            swap_out[sub * 64 : sub * 64 + 64, :] = total[i * 64 : i * 64 + 64].astype(BF16)
            view = pl.ds(sub * 64, 64)
            move("swap", ("swap", sub), swap_out.at[view], swap_in.at[view], hi_peer)
        stay = res[4 * wave : 4 * wave + 4].reshape(128, DZ).astype(F32)
        hidden[wave * 128 : wave * 128 + 128, :] = total[128:] + stay

    partial[0] = project(0, 0) + project(1, 0) + project(2, 0)
    accumulate(0, 3, 4)
    accumulate(0, 5, 6)
    own_res.wait()
    load_gain.wait()
    arrived(res.at[pl.ds(0, NZ - 1)], "res")
    wait_heads(3, 0)
    swap(0)
    gather_heads(2, 3)
    partial[1] = project(0, 1) + project(1, 1) + project(2, 1)
    last_heads(1)
    fetch_1(3)
    fetch_1(4)
    fetch_1(5)
    accumulate(1, 3, 4)

    def sub_rows(sub):
        return pl.ds(sub * 64, 64)

    def wait_hidden(step, key):
        arrived(slices.at[0, pl.ds(0, 128)], "hidden", step, key)

    def send_hidden(way, step, sub, key):
        src = slices.at[GATHER_FROM[way][step], sub_rows(sub)]
        dst = slices.at[GATHER_TO[way][step], sub_rows(sub)]
        move("hidden", ("hidden", step, key), src, dst, z_peer[1 if way == 0 else -1])

    def gather_hidden(step, sub):
        if step > 0:
            wait_hidden(step - 1, sub)
        for way in range(2):
            send_hidden(way, step, sub, sub)

    def last_hidden(wave):
        for way in range(2):
            wait_hidden(2, 2 * wave + way)
            send_hidden(way, 3, 2 * wave + way, wave)

    def finish(sub):
        arrived(swap_in.at[pl.ds(0, 64)], "swap", sub)
        rows = slice(sub * 64, (sub + 1) * 64)
        value = hidden[rows, :] + swap_in[rows, :].astype(F32)
        hidden[rows, :] = value
        slices[0, rows, :] = (value * gain_ref[...]).astype(BF16)
        gather_hidden(0, sub)

    own_tiles = (slice(0, 256), slice(256, 512), slice(512, 640))
    other_tiles = (slice(640, 896), slice(896, 1152), slice(1152, 1280))
    all_tiles = tuple(slice(i * TILE, (i + 1) * TILE) for i in range(5))

    def multiply(slots, low, high, cols, more=True):
        value = logits[low:high, cols] if more else 0.0
        for slot in slots:
            deep = pl.ds(pl.multiple_of(along_z(SLOT_OFFSET[slot]) * DZ, DZ), DZ)
            value = value + dot(slices[slot, low:high, :], wh[deep, cols])
        logits[low:high, cols] = value

    finish(0)
    finish(1)
    accumulate(1, 5, 6)
    wait_heads(3, 1)
    swap(1)
    gather_hidden(1, 0)
    finish(2)
    gather_hidden(1, 1)
    finish(3)
    square = jnp.sum(hidden[...] * hidden[...], axis=1, keepdims=True)
    turned = jnp.broadcast_to(square, (HALF, HD)).T
    squares[0] = jnp.concatenate(
        [turned[0:1, 0:HD], turned[0:1, HD:HALF], jnp.zeros((6, HD), F32)], axis=0
    )
    for slot in range(1, NZ):
        offset = SLOT_OFFSET[slot]
        peer = z_peer[offset if slot == NZ - 1 else -offset]
        move("square", ("square",), squares.at[0], squares.at[slot], peer)

    own_offset = vocab * NV
    other_offset = (z * 2 + 1 - x_hi) * NV

    def summarize(low, high):
        size = high - low
        values = logits[low:high, :] * factor[low:high]
        top = jnp.max(values, axis=1, keepdims=True)
        mass = jnp.sum(jnp.exp(values - top), axis=1, keepdims=True)
        column = lax.broadcasted_iota(jnp.int32, (size, 2 * NV), 1)
        column = jnp.where(column < NV, column + own_offset, column - NV + other_offset)
        goal = goals[low:high, 3:4].astype(jnp.int32)
        hit = jnp.sum(jnp.where(column == goal, values, 0.0), axis=1, keepdims=True)
        lane_of = lax.broadcasted_iota(jnp.int32, (size, HD), 1)
        stats[low:high, :] = jnp.where(lane_of == 0, top, jnp.where(lane_of == 1, mass, hit))

    own_wh.wait()
    fetch_2(0)
    for tile in own_tiles:
        multiply((0,), 0, HALF, tile, False)
    gather_hidden(1, 2)
    fetch_2(1)
    fetch_2(2)
    gather_hidden(1, 3)
    fetch_2(3)
    for tile in own_tiles:
        multiply((1, 2), 0, HALF, tile)
    gather_hidden(2, 0)
    fetch_2(4)
    gather_hidden(2, 1)
    fetch_2(5)
    gather_hidden(2, 2)
    fetch_3(1)
    fetch_3(2)
    fetch_3(3)
    gather_hidden(2, 3)
    fetch_3(4)
    fetch_3(5)
    for tile in own_tiles:
        multiply((3, 4), 0, HALF, tile)
    last_hidden(0)
    fetch_4()
    for tile in other_tiles:
        multiply((0, 1, 2, 3, 4), 0, HALF, tile, False)
    last_hidden(1)
    total_square = squares[0]
    arrived(squares.at[pl.ds(0, NZ - 1)], "square")
    for slot in range(1, NZ):
        total_square = total_square + squares[slot]
    factor = lax.rsqrt(total_square / D + EPSILON)
    factor = jnp.concatenate([factor, jnp.zeros((HD - 8, HD), F32)], axis=0).T
    factor = jnp.concatenate([factor[:, 0:1], factor[:, 1:2]], axis=0)
    for tile in all_tiles:
        multiply((5, 6), 0, HALF, tile)
    for i in range(2):
        wait_hidden(3, i)
        for tile in all_tiles:
            multiply((7,), i * 128, i * 128 + 128, tile)
        summarize(i * 128, i * 128 + 128)
    turned = stats[...].T
    for half in range(2):
        stats_out[half] = turned[0:8, half * HD : (half + 1) * HD]
    for by in (4, 3, -3, 2, -2, 1, -1):
        move("stats", ("stats",), stats_out.at[along_z(by) // 4], stats_in.at[by + 3], z_peer[by])
    blocks = [stats_out[z // 4]]
    arrived(stats_in.at[pl.ds(0, NZ - 1)], "stats")
    for by in OTHERS:
        blocks.append(stats_in[by + 3])
    top = blocks[0][0:1]
    for block in blocks[1:]:
        top = jnp.maximum(top, block[0:1])
    mass = jnp.zeros((1, HD), F32)
    hit = jnp.zeros((1, HD), F32)
    for block in blocks:
        mass = mass + block[1:2] * jnp.exp(block[0:1] - top)
        hit = hit + block[2:3]
    result = hit - top - jnp.log(mass)
    quarter = lax.rem(z, 4)
    picked = result[:, 0:CH]
    for i in range(1, 4):
        picked = jnp.where(quarter == i, result[:, i * CH : (i + 1) * CH], picked)
    out_ref[...] = picked
    departed(state_in, "state")
    departed(res.at[pl.ds(0, NZ - 1)], "res")
    departed(wo.at[0, pl.ds(0, 15)], "strip")
    departed(wo.at[pl.ds(0, NZ - 1)], "wo")
    departed(wh_rows(D), "wh")
    departed(heads.at[pl.ds(0, NZ - 1)], "heads")
    departed(swap_out, "swap")
    departed(slices.at[pl.ds(0, NZ - 1)], "hidden")
    departed(squares.at[pl.ds(0, NZ - 1)], "square")
    departed(stats_in.at[pl.ds(0, NZ - 1)], "stats")


def shards(
    query_rows, key_rows, value_rows, log_decay, segment_ids, residual, out_weight, final_gain,
    head_weight, targets,
):
    vmem = pl.BlockSpec(memory_space=pltpu.VMEM)
    hbm = pl.BlockSpec(memory_space=pl.ANY)
    dma = pltpu.SemaphoreType.DMA
    result = pl.pallas_call(
        kernel,
        out_shape=jax.ShapeDtypeStruct((1, CH), F32),
        in_specs=[hbm] * 10,
        out_specs=vmem,
        scratch_shapes=[
            pltpu.VMEM((TOK, 2 * HD), BF16),
            pltpu.VMEM((TOK, 2 * HD), BF16),
            pltpu.VMEM((TOK, 2 * HD), BF16),
            pltpu.VMEM((2, TOK), F32),
            pltpu.VMEM((1, TOK), jnp.int32),
            pltpu.VMEM((1, TOK), jnp.int32),
            pltpu.VMEM((NZ, CH, DZ), BF16),
            pltpu.VMEM((1, DZ), F32),
            pltpu.VMEM((NZ, 16, 16, DZ), BF16),
            pltpu.VMEM((D, 2 * NV), BF16),
            pltpu.VMEM((2, HALF, 2 * HD), BF16),
            pltpu.VMEM((NZ, 4, 128, 2 * HD), BF16),
            pltpu.VMEM((2, HALF, DZ), F32),
            pltpu.VMEM((HALF, DZ), F32),
            pltpu.VMEM((HALF, DZ), BF16),
            pltpu.VMEM((HALF, DZ), BF16),
            pltpu.VMEM((NZ, HALF, DZ), BF16),
            pltpu.VMEM((HALF, 2 * NV), F32),
            pltpu.VMEM((NZ, 8, HD), F32),
            pltpu.VMEM((2, TOK, HD), F32),
            pltpu.VMEM((TOK, HD), F32),
            pltpu.VMEM((HALF, HD), F32),
            pltpu.VMEM((3, 2 * HD + 16, HD), BF16),
            pltpu.VMEM((5, 2 * HD + 16, HD), BF16),
            pltpu.VMEM((HALF, HD), F32),
            pltpu.VMEM((2, 8, HD), F32),
            pltpu.VMEM((NZ, 8, HD), F32),
            dma((10,)),
            dma((len(GROUPS),)),
            dma((ARRIVALS,)),
        ],
        compiler_params=pltpu.CompilerParams(
            collective_id=0, has_side_effects=True, vmem_limit_bytes=56 * 1024 * 1024
        ),
        name="layer",
    )(
        query_rows, key_rows, value_rows, log_decay, segment_ids.reshape(1, -1),
        targets.reshape(1, -1), residual, final_gain.reshape(1, -1), out_weight, head_weight,
    )
    return result.reshape(CH)


def solution(mesh):
    in_specs = (
        P("ctx", "vocab"),
        P("ctx", "vocab"),
        P("ctx", "vocab"),
        P("vocab", "ctx"),
        P("ctx"),
        P(("ctx", "vocab"), None),
        P("vocab", None),
        P(),
        P(None, "vocab"),
        P("ctx"),
    )
    out_specs = P(("ctx", "vocab"))
    return jax.shard_map(shards, mesh=mesh, in_specs=in_specs, out_specs=out_specs, check_vma=False)
```

time: 90.4 us -> 85.5 us (0.946)
  Pallas kernels: 88.6 us -> 84.2 us
    pallas_call x1, Pallas kernels: 88.6 us -> 84.2 us  [shards(): pl.pallas_call(kernel, out_shape=jax.ShapeDtypeStruct((1, CH), F32), in_s...]
where the time goes in v4:
time: 85.5 us; the launch traced here: 85.4 us
  Pallas kernels  84.2 us (98%)
  local copies, waits for them, and re-layouts  1.19 us (1%)
    pallas_call x1, Pallas kernels, shards(): pl.pallas_call(kernel, out_shape=jax.ShapeDtypeStruct((1, CH), F32), in_s...  84.2 us

profile of v4, /device:TPU:24, one launch (start us, length us, event | category | flops | bytes accessed | tf_op | source)
XLA Modules:
  0.0 85.4 jit_solution(3390255194366800369)
XLA Ops:
  0.0 84.2 %layer.1 = f32[1,32]{1,0:T(1,128)} custom-call(bf16[512,256]{1,0:T(8,128)(2,1)} %q_hbm.1, bf16[512,256]{1,0:T(8,128)(2,1)} %k_hbm.1, bf16[512,256]{1,0:T(8,128)(2,1)} %v_hbm.1, f32[2,512]{1,0:T(2,128)} %ld_hbm.1, s32[1,512]{1,0:T(1,128)} %bitcast.5, s32[1,512]{1,0:T(1,128)} %bitcast.6, bf16[32,6144]{1,0:T(8,128)(2,1)} %res_hbm.1, f32[1,6144]{1,0:T(1,128)} %bitcast.4, ...), custom_call_target="tpu_custom_call" | custom-call | tf_op jit(solution)/shard_map/layer/pallas_call | solution.py:615
  84.2 1.2 %copy.12 = f32[32]{0:T(128)} copy(f32[32]{0:T(128)} %bitcast.7) | data formatting | bytes 256

commit v5 on v4

--- a/solution.py
+++ b/solution.py
@@ -22,7 +22,10 @@
 ARRIVALS = 65
 GROUPS = ("state", "res", "strip", "wo", "wh", "heads", "swap", "hidden", "square", "stats")
 
+STATE = 144
+CHIPS = ((0, -1), (0, 1), (0, 2), (1, 0), (1, -1), (1, 1), (1, 2))
 OTHERS = (1, -1, 2, -2, 3, -3, 4)
+EARLY = 6
 SLOT_OFFSET = (0, -1, 1, -2, 2, -3, 3, 4)
 GATHER_FROM = ((0, 1, 3, 5), (0, 2, 4, 6))
 GATHER_TO = ((1, 3, 5, 7), (2, 4, 6, 7))
@@ -60,12 +63,16 @@
     sibling = (ctx + 1 - 2 * core, vocab)
     y_peer = {by: (at_y(by), vocab) for by in (-1, 1, 2)}
     lo_peer = (lax.rem(ctx + 8, 16), vocab)
+    chip_peer = {
+        (lo, by): (lax.rem(x_lo + lo, 2) * 8 + lax.rem(y + by + 4, 4) * 2 + core, vocab)
+        for lo, by in CHIPS
+    }
     cut_peer = (lax.rem(ctx + 8, 16), z * 2 + 1 - x_hi)
     hi_peer = (ctx, z * 2 + 1 - x_hi)
     z_peer = {by: (ctx, along_z(by) * 2 + x_hi) for by in (-3, -2, -1, 1, 2, 3, 4)}
 
     barrier = pltpu.get_barrier_semaphore()
-    peers = [sibling, lo_peer, cut_peer, hi_peer, *y_peer.values(), *z_peer.values()]
+    peers = [sibling, cut_peer, hi_peer, *chip_peer.values(), *z_peer.values()]
     for peer in peers:
         pl.semaphore_signal(barrier, inc=1, device_id=peer, device_id_type=MESH)
 
@@ -250,45 +257,43 @@
         own_state.append(summary)
         decay.append(jnp.exp(last))
 
-    def pack(slot, states, decays, seg):
-        for h in range(2):
-            state_out[slot, h * HD : (h + 1) * HD, :] = states[h].astype(BF16)
+    def pack(start, state, falloff, seg):
+        state_out[start : start + HD, :] = state.astype(BF16)
         row = lax.broadcasted_iota(jnp.int32, (16, HD), 0)
-        tops = [d.astype(BF16).astype(F32) for d in decays]
-        block = jnp.where(row == 0, tops[0], 0.0)
-        block = jnp.where(row == 1, decays[0] - tops[0], block)
-        block = jnp.where(row == 2, tops[1], block)
-        block = jnp.where(row == 3, decays[1] - tops[1], block)
-        block = jnp.where(row == 4, seg, block)
-        state_out[slot, 2 * HD : 2 * HD + 16, :] = block.astype(BF16)
-
-    def unpack(buffer, slot):
-        states = [buffer[slot, h * HD : (h + 1) * HD, :].astype(F32) for h in range(2)]
-        block = buffer[slot, 2 * HD : 2 * HD + 16, :].astype(F32)
-        decays = [block[0:1, 0:1] + block[1:2, 0:1], block[2:3, 0:1] + block[3:4, 0:1]]
-        return states, decays, block[4:5, 0:1]
+        high = falloff.astype(BF16).astype(F32)
+        block = jnp.where(row == 0, high, jnp.where(row == 1, falloff - high, 0.0))
+        block = jnp.where(row == 2, seg, block)
+        state_out[start + HD : start + STATE, :] = block.astype(BF16)
+
+    def unpack(start):
+        block = state_in[start + HD : start + STATE, :].astype(F32)
+        return (
+            state_in[start : start + HD, :].astype(F32),
+            block[0:1, 0:1] + block[1:2, 0:1],
+            block[2:3, 0:1],
+        )
 
     def join(first, second):
-        states = [
-            jnp.where(first[2] == second[2], second[1][h], 0.0) * first[0][h] + second[0][h]
-            for h in range(2)
-        ]
-        return states, [first[1][h] * second[1][h] for h in range(2)], second[2]
+        state = jnp.where(first[2] == second[2], second[1], 0.0) * first[0] + second[0]
+        return state, first[1] * second[1], second[2]
 
     def choose(flag, a, b):
-        return (
-            [jnp.where(flag, a[0][h], b[0][h]) for h in range(2)],
-            [jnp.where(flag, a[1][h], b[1][h]) for h in range(2)],
-            jnp.where(flag, a[2], b[2]),
-        )
-
-    pack(0, own_state, decay, seg_last)
+        return tuple(jnp.where(flag, one, other) for one, other in zip(a, b))
+
+    def of_head(h):
+        return own_state[h], decay[h], seg_last
+
+    pack(0, *choose(core == 0, of_head(1), of_head(0)))
+    def send_res(offsets):
+        for by in offsets:
+            cols = pl.ds(pl.multiple_of(along_z(by) * DZ, 128), DZ)
+            move("res", ("res",), res_hbm.at[:, cols], res.at[z], z_peer[by])
+
     pl.semaphore_wait(barrier, len(peers))
-    move("state", ("state_core",), state_out.at[0], state_in.at[0], sibling)
+    rows = pl.ds(0, STATE)
+    move("state", ("state_core",), state_out.at[rows], state_in.at[rows], sibling)
     own_strip_copy = wo_0()
-    for by in OTHERS:
-        cols = pl.ds(pl.multiple_of(along_z(by) * DZ, 128), DZ)
-        move("res", ("res",), res_hbm.at[:, cols], res.at[z], z_peer[by])
+    send_res(OTHERS[:EARLY])
     for piece in range(len(KINDS)):
         fetch_0(piece)
     cols = pl.ds(pl.multiple_of(z * DZ, 128), DZ)
@@ -313,49 +318,53 @@
             mixing = (scores * weights).astype(BF16)
             within[h, low:high, :] = dot(mixing, v_ref[0:high, head])
 
-    arrived(state_in.at[0], "state_core")
+    arrived(state_in.at[pl.ds(0, STATE)], "state_core")
     own_wh = load(9, wh_ref, wh.at[:, pl.ds(0, NV)])
-
-    own = (own_state, decay, seg_last)
-    other = unpack(state_in, 0)
+    own = choose(core == 0, of_head(0), of_head(1))
+    other = unpack(0)
     first = choose(core == 0, own, other)
     second = choose(core == 0, other, own)
     chip = join(first, second)
-    pack(1, *chip)
-    for index, by in enumerate((-1, 1, 2)):
-        move("state", ("state_y",), state_out.at[1], state_in.at[1 + index], y_peer[by])
+    pack(STATE, *chip)
+    for index, peer in enumerate(CHIPS):
+        src = state_out.at[pl.ds(STATE, STATE)]
+        dst = state_in.at[pl.ds((1 + index) * STATE, STATE)]
+        move("state", ("chips",), src, dst, chip_peer[peer])
     load_q.wait()
     inside(0)
     inside(1)
-    arrived(state_in.at[pl.ds(1, 3)], "state_y")
-    chips = {0: chip}
-    for index, by in enumerate((1, -1, 2)):
-        chips[by] = unpack(state_in, 1 + index)
+    arrived(state_in.at[pl.ds(STATE, len(CHIPS) * STATE)], "chips")
+    chips = {(0, 0): chip}
+    for index, (lo, by) in enumerate(CHIPS):
+        chips[lo, by if by in (0, 2) else -by] = unpack((1 + index) * STATE)
 
     def chip_at(target):
-        picked = chips[0]
-        for by in (1, -1, 2):
-            picked = choose(lax.rem(y + by + 4, 4) == target, chips[by], picked)
+        picked = chip
+        for (lo, by), value in chips.items():
+            if (lo, by) != (0, 0):
+                number = lax.rem(x_lo + lo, 2) * 4 + lax.rem(y + by + 4, 4)
+                picked = choose(number == target, value, picked)
         return picked
 
-    nothing = ([jnp.zeros((HD, HD), F32)] * 2, [jnp.ones((1, 1), F32)] * 2, jnp.zeros((1, 1), F32))
+    my_chip = x_lo * 4 + y
     total = chip_at(0)
-    before = choose(y == 0, nothing, total)
-    for target in range(1, 4):
+    before = choose(my_chip == 0, (jnp.zeros((HD, HD), F32),) + chip[1:], total)
+    for target in range(1, 7):
         total = join(total, chip_at(target))
-        before = choose(y > target, total, before)
-    pack(2, *total)
-    move("state", ("total",), state_out.at[2], state_in.at[4], lo_peer)
+        before = choose(my_chip > target, total, before)
+    inner = choose(my_chip == 0, first, join(before, first))
+    mine = choose(core == 0, before, inner)
+    others = choose(core == 0, inner, before)
+    prior = mine[2]
+    state_out[2 * STATE : 2 * STATE + HD, :] = others[0].astype(BF16)
+    last_rows = pl.ds(8 * STATE, HD)
+    move(
+        "state", ("incoming",), state_out.at[pl.ds(2 * STATE, HD)], state_in.at[last_rows], sibling
+    )
     wo_1()
-    arrived(state_in.at[4], "total")
-    earlier = unpack(state_in, 4)
-    joined = choose(y == 0, earlier, join(earlier, before))
-    before = choose(x_lo == 0, before, joined)
-    fresh = (x_lo == 0) & (y == 0)
-    with_first = choose(fresh, first, join(before, first))
-    before = choose(core == 0, before, with_first)
-    prior = before[2]
-
+    arrived(state_in.at[last_rows], "incoming")
+    received = state_in[8 * STATE : 8 * STATE + HD, :].astype(F32)
+    incoming = [jnp.where(core == h, mine[0], received).astype(BF16) for h in range(2)]
 
     def own_heads(sub):
         return attn.at[x_hi if sub % 2 else 1 - x_hi, pl.ds(sub // 2 * 128, 128)]
@@ -382,7 +391,7 @@
     for h in range(2):
         head = slice(h * HD, (h + 1) * HD)
         scale = jnp.where(seg_col == prior, jnp.exp(columns[:, h : h + 1]), 0.0)
-        carried = dot(q_ref[:, head], before[0][h].astype(BF16))
+        carried = dot(q_ref[:, head], incoming[h])
         output = within[h] + scale * carried
         mean = jnp.mean(output * output, axis=-1, keepdims=True)
         scaled = (output * lax.rsqrt(mean + EPSILON)).astype(BF16)
@@ -390,27 +399,28 @@
             for half in range(2):
                 low = (2 * j + half) * CH
                 attn[half, j * CH : (j + 1) * CH, head] = scaled[low : low + CH]
-    for sub in range(3):
+    for sub in range(2):
         gather_heads(0, sub)
+    gather_heads(1, 0)
+    gather_heads(1, 1)
+    gather_heads(0, 2)
     wo_2()
     wo_3()
     for j in range(NZ):
         rows = pl.ds(pl.multiple_of((2 * j + x_hi) * CH, CH), CH)
         goals[j * CH : (j + 1) * CH, :] = columns[rows, :]
-    gather_heads(1, 0)
-    gather_heads(1, 1)
+    gather_heads(2, 0)
     gather_heads(0, 3)
-    gather_heads(2, 0)
     gather_heads(2, 1)
+    gather_heads(1, 2)
     wo_4()
-    gather_heads(1, 2)
     fetch_1(0)
+    gather_heads(1, 3)
+    last_heads(0)
     wo_5()
-    last_heads(0)
-    gather_heads(1, 3)
+    gather_heads(2, 2)
     fetch_1(1)
     fetch_1(2)
-    gather_heads(2, 2)
     wo_6()
 
     def project(slot, wave):
@@ -433,18 +443,15 @@
             swap_out[sub * 64 : sub * 64 + 64, :] = total[i * 64 : i * 64 + 64].astype(BF16)
             view = pl.ds(sub * 64, 64)
             move("swap", ("swap", sub), swap_out.at[view], swap_in.at[view], hi_peer)
-        stay = res[4 * wave : 4 * wave + 4].reshape(128, DZ).astype(F32)
-        hidden[wave * 128 : wave * 128 + 128, :] = total[128:] + stay
+        hidden[wave * 128 : wave * 128 + 128, :] = total[128:]
 
     partial[0] = project(0, 0) + project(1, 0) + project(2, 0)
     accumulate(0, 3, 4)
     accumulate(0, 5, 6)
-    own_res.wait()
-    load_gain.wait()
-    arrived(res.at[pl.ds(0, NZ - 1)], "res")
+    gather_heads(2, 3)
     wait_heads(3, 0)
     swap(0)
-    gather_heads(2, 3)
+    send_res(OTHERS[EARLY:])
     partial[1] = project(0, 1) + project(1, 1) + project(2, 1)
     last_heads(1)
     fetch_1(3)
@@ -478,6 +485,7 @@
         arrived(swap_in.at[pl.ds(0, 64)], "swap", sub)
         rows = slice(sub * 64, (sub + 1) * 64)
         value = hidden[rows, :] + swap_in[rows, :].astype(F32)
+        value = value + res[2 * sub : 2 * sub + 2].reshape(64, DZ).astype(F32)
         hidden[rows, :] = value
         slices[0, rows, :] = (value * gain_ref[...]).astype(BF16)
         gather_hidden(0, sub)
@@ -493,6 +501,9 @@
             value = value + dot(slices[slot, low:high, :], wh[deep, cols])
         logits[low:high, cols] = value
 
+    own_res.wait()
+    load_gain.wait()
+    arrived(res.at[pl.ds(0, NZ - 1)], "res")
     finish(0)
     finish(1)
     accumulate(1, 5, 6)
@@ -640,8 +651,8 @@
             pltpu.VMEM((2, TOK, HD), F32),
             pltpu.VMEM((TOK, HD), F32),
             pltpu.VMEM((HALF, HD), F32),
-            pltpu.VMEM((3, 2 * HD + 16, HD), BF16),
-            pltpu.VMEM((5, 2 * HD + 16, HD), BF16),
+            pltpu.VMEM((2 * STATE + HD, HD), BF16),
+            pltpu.VMEM((8 * STATE + HD, HD), BF16),
             pltpu.VMEM((HALF, HD), F32),
             pltpu.VMEM((2, 8, HD), F32),
             pltpu.VMEM((NZ, 8, HD), F32),

time: 85.5 us -> 85.2 us (level)
  no operation moved by 1% of the time
where the time goes in v5:
time: 85.2 us; the launch traced here: 85.1 us
  Pallas kernels  83.9 us (98%)
  local copies, waits for them, and re-layouts  1.19 us (1%)
    pallas_call x1, Pallas kernels, shards(): pl.pallas_call(kernel, out_shape=jax.ShapeDtypeStruct((1, CH), F32), in_s...  83.9 us

profile of v5, /device:TPU:24, one launch (start us, length us, event | category | flops | bytes accessed | tf_op | source)
XLA Modules:
  0.0 85.1 jit_solution(11973125476095710690)
XLA Ops:
  0.0 83.9 %layer.1 = f32[1,32]{1,0:T(1,128)} custom-call(bf16[512,256]{1,0:T(8,128)(2,1)} %q_hbm.1, bf16[512,256]{1,0:T(8,128)(2,1)} %k_hbm.1, bf16[512,256]{1,0:T(8,128)(2,1)} %v_hbm.1, f32[2,512]{1,0:T(2,128)} %ld_hbm.1, s32[1,512]{1,0:T(1,128)} %bitcast.5, s32[1,512]{1,0:T(1,128)} %bitcast.6, bf16[32,6144]{1,0:T(8,128)(2,1)} %res_hbm.1, f32[1,6144]{1,0:T(1,128)} %bitcast.4, ...), custom_call_target="tpu_custom_call" | custom-call | tf_op jit(solution)/shard_map/layer/pallas_call | solution.py:626
  83.9 1.2 %copy.12 = f32[32]{0:T(128)} copy(f32[32]{0:T(128)} %bitcast.7) | data formatting | bytes 256

commit v6 on v5

--- a/solution.py
+++ b/solution.py
@@ -563,10 +563,10 @@
     for tile in own_tiles:
         multiply((3, 4), 0, HALF, tile)
     last_hidden(0)
+    last_hidden(1)
     fetch_4()
     for tile in other_tiles:
         multiply((0, 1, 2, 3, 4), 0, HALF, tile, False)
-    last_hidden(1)
     total_square = squares[0]
     arrived(squares.at[pl.ds(0, NZ - 1)], "square")
     for slot in range(1, NZ):

time: 85.2 us -> 86.6 us (1.016)
  Pallas kernels: 83.9 us -> 85.3 us
    pallas_call x1, Pallas kernels: 83.9 us -> 85.3 us  [shards(): pl.pallas_call(kernel, out_shape=jax.ShapeDtypeStruct((1, CH), F32), in_s...]
where the time goes in v6:
time: 86.6 us; the launch traced here: 86.5 us
  Pallas kernels  85.3 us (98%)
  local copies, waits for them, and re-layouts  1.19 us (1%)
    pallas_call x1, Pallas kernels, shards(): pl.pallas_call(kernel, out_shape=jax.ShapeDtypeStruct((1, CH), F32), in_s...  85.3 us

profile of v6, /device:TPU:24, one launch (start us, length us, event | category | flops | bytes accessed | tf_op | source)
XLA Modules:
  0.0 86.5 jit_solution(1241074380678655235)
XLA Ops:
  0.0 85.3 %layer.1 = f32[1,32]{1,0:T(1,128)} custom-call(bf16[512,256]{1,0:T(8,128)(2,1)} %q_hbm.1, bf16[512,256]{1,0:T(8,128)(2,1)} %k_hbm.1, bf16[512,256]{1,0:T(8,128)(2,1)} %v_hbm.1, f32[2,512]{1,0:T(2,128)} %ld_hbm.1, s32[1,512]{1,0:T(1,128)} %bitcast.5, s32[1,512]{1,0:T(1,128)} %bitcast.6, bf16[32,6144]{1,0:T(8,128)(2,1)} %res_hbm.1, f32[1,6144]{1,0:T(1,128)} %bitcast.4, ...), custom_call_target="tpu_custom_call" | custom-call | tf_op jit(solution)/shard_map/layer/pallas_call | solution.py:626
  85.3 1.2 %copy.12 = f32[32]{0:T(128)} copy(f32[32]{0:T(128)} %bitcast.7) | data formatting | bytes 256
